TPU v7x, 32 devices: a whole 2x2x4 slice. The times are simulated.
32 devices in a mesh: seq: 8 (over z, x), head: 4 (over y, core).
Axes of the slice: x: 2, y: 2, z: 4, core: 2. Of those that a mesh axis runs over, the one named last changes fastest.
Arguments:
- queries: bfloat16 [1024, 4096], P(('seq', 'head')), may hold values from -6 to 6
- keys: bfloat16 [1024, 4096], P(('seq', 'head')), may hold values from -6 to 6
- values: bfloat16 [1024, 4096], P(('seq', 'head')), may hold values from -6 to 6
- grad_out: bfloat16 [1024, 4096], P(('seq', 'head')), may hold values from -6 to 6
- random_blocks: int32 [32, 16, 3], replicated, may hold values from 0 to 15, as said below
- global_blocks: int32 [2], replicated, may hold values from 0 to 15
Outputs:
- attended: bfloat16 [1024, 4096], P(('seq', 'head'))
- grad_queries: bfloat16 [1024, 4096], P(('seq', 'head'))
- grad_keys: bfloat16 [1024, 4096], P(('seq', 'head'))
- grad_values: bfloat16 [1024, 4096], P(('seq', 'head'))
Inputs may be any that keep to these rules, and one draw needn't show every extreme that they name: `random_blocks`: for the heads of one index of head and the query blocks of one index of seq, at most 7 random entries lie in the blocks of any one index of seq, and in every such group some index of seq holds exactly 7.
All inputs are finite; a program needn't handle non-finite values.
Results may differ from a plain program's by a relative error of at most 0.034.
Values may be sent and summed in bfloat16 or wider, within the bound.
No kernel may reach another device: no remote copies, remote signals or barrier semaphores. Data moves between devices by JAX's collectives and lax.ppermute only.
A program may use at most 128 MiB of HBM per device.

v0:
```python
import jax
import jax.numpy as jnp
from jax import lax
from jax.sharding import PartitionSpec as P

HEAD_DIM = 128
BLOCK = 64
RAND_BLOCKS = 3
GLOB_BLOCKS = 2


def extended(shard, sides, width):
    for axis, dim in sides:
        devices, length = (lax.axis_size(axis), shard.shape[dim])
        up = [(i, (i + 1) % devices) for i in range(devices - 1)]
        down = [(j, i) for i, j in up]
        last = lax.slice_in_dim(shard, length - width, length, axis=dim)
        first = lax.slice_in_dim(shard, 0, width, axis=dim)
        before = lax.ppermute(last, axis, up)
        after = lax.ppermute(first, axis, down)
        shard = jnp.concatenate([before, shard, after], axis=dim)
    return shard


def spread_2(shard, axis, root):
    mine = lax.axis_index(axis) == root
    return lax.psum(jnp.where(mine, shard, jnp.zeros_like(shard)), axis)


def product(formula, former, latter):
    return jnp.einsum(formula, former, latter, preferred_element_type=jnp.float32)


def spread(near_part, offset):
    widths = [(0, 0), (offset, 2 - offset), (0, 0), (0, 0), (0, 0)]
    return jnp.pad(near_part, widths)


def body(queries, keys, values, grad_out, random_blocks, global_blocks):
    score_scale = HEAD_DIM ** (-0.5)
    query_rows, key_rows, value_rows, upstream_rows = (
        lax.all_to_all(queries, "head", split_axis=1, concat_axis=0, tiled=True),
        lax.all_to_all(keys, "head", split_axis=1, concat_axis=0, tiled=True),
        lax.all_to_all(values, "head", split_axis=1, concat_axis=0, tiled=True),
        lax.all_to_all(grad_out, "head", split_axis=1, concat_axis=0, tiled=True),
    )
    tokens_here, width_here = query_rows.shape
    heads_here = width_here // HEAD_DIM
    blocks_here = tokens_here // BLOCK
    shards = lax.axis_size("seq")
    my_shard = lax.axis_index("seq")
    my_group = lax.axis_index("head")
    tile_shape = (blocks_here, BLOCK, heads_here, HEAD_DIM)
    query_tiles = query_rows.reshape(tile_shape)
    incoming_gradient = upstream_rows.reshape(tile_shape)
    pair_rows = jnp.stack([key_rows, value_rows])
    widened = extended(pair_rows, (("seq", 1),), BLOCK)
    widened = widened.reshape((2, blocks_here + 2) + tile_shape[1:])
    window = jnp.stack([widened[:, :-2], widened[:, 1:-1], widened[:, 2:]], axis=2)
    total_blocks = shards * blocks_here
    block_ids = my_shard * blocks_here + jnp.arange(blocks_here, dtype=jnp.int32)
    window_ok = jnp.stack([block_ids >= 1, block_ids >= 0, block_ids + 1 < total_blocks], axis=1)
    pair_tiles = pair_rows.reshape((2,) + tile_shape)
    fetched = []
    for glob_index in range(GLOB_BLOCKS):
        target = global_blocks[glob_index]
        global_tile = lax.dynamic_index_in_dim(pair_tiles, target % blocks_here, 1, keepdims=False)
        fetched.append(spread_2(global_tile, "seq", target // blocks_here))
    global_pair = jnp.stack(fetched, axis=1)
    requests = heads_here * blocks_here * RAND_BLOCKS
    slot_count = max(2, requests // shards + 1)
    request_table = lax.dynamic_slice_in_dim(random_blocks, my_group * heads_here, heads_here, 0)
    request_table = (
        request_table.reshape(heads_here, shards, blocks_here, RAND_BLOCKS)
        .transpose(1, 0, 2, 3)
        .reshape(shards, requests)
    )
    owners = request_table // blocks_here
    positions = jnp.arange(requests, dtype=jnp.int32)
    tile_ids = positions // (blocks_here * RAND_BLOCKS) * blocks_here + request_table % blocks_here
    to_me = (owners == my_shard).astype(jnp.int32)
    order_out = jnp.cumsum(to_me, axis=1) - to_me
    slot_ids = jnp.arange(slot_count, dtype=jnp.int32)
    chosen = (to_me[:, None, :] == 1) & (order_out[:, None, :] == slot_ids[None, :, None])
    slot_used = jnp.any(chosen, axis=2)
    send_ids = jnp.sum(jnp.where(chosen, tile_ids[:, None, :], 0), axis=2)
    send_block = send_ids % blocks_here
    send_head = send_ids // blocks_here
    slot_mask = slot_used[:, :, None, None]
    key_send = jnp.where(
        slot_mask, pair_tiles[0][send_block, :, send_head, :], jnp.zeros((), jnp.bfloat16)
    )
    value_send = jnp.where(
        slot_mask, pair_tiles[1][send_block, :, send_head, :], jnp.zeros((), jnp.bfloat16)
    )
    key_recv, value_recv = (
        lax.all_to_all(key_send, "seq", split_axis=0, concat_axis=0, tiled=True),
        lax.all_to_all(value_send, "seq", split_axis=0, concat_axis=0, tiled=True),
    )
    my_table = lax.dynamic_index_in_dim(request_table, my_shard, 0, keepdims=False)
    my_owner = my_table // blocks_here
    by_owner = (my_owner[:, None] == jnp.arange(shards, dtype=jnp.int32)[None, :]).astype(jnp.int32)
    my_slot = jnp.sum((jnp.cumsum(by_owner, axis=0) - by_owner) * by_owner, axis=1)
    rand_shape = (heads_here, blocks_here, RAND_BLOCKS, BLOCK, HEAD_DIM)
    rand_keys = key_recv[my_owner, my_slot].reshape(rand_shape)
    rand_values = value_recv[my_owner, my_slot].reshape(rand_shape)
    attention_logits = (
        jnp.concatenate(
            [
                product("iahd,ijbhd->hiajb", query_tiles, window[0]),
                product("iahd,jbhd->hiajb", query_tiles, global_pair[0]),
                product("iahd,hijbd->hiajb", query_tiles, rand_keys),
            ],
            axis=3,
        )
        * score_scale
    )
    key_valid = jnp.concatenate(
        [window_ok, jnp.ones((blocks_here, GLOB_BLOCKS + RAND_BLOCKS), bool)], axis=1
    )
    attention_logits = jnp.where(key_valid[None, :, None, :, None], attention_logits, -jnp.inf)
    row_max = jnp.max(attention_logits, axis=(3, 4), keepdims=True)
    exponent = jnp.exp(attention_logits - row_max)
    row_sum = jnp.sum(exponent, axis=(3, 4), keepdims=True)
    probability = exponent / row_sum
    attention_weight = probability.astype(jnp.bfloat16)
    split_at = 3 + GLOB_BLOCKS
    weight_win = attention_weight[:, :, :, :3]
    weight_glob = attention_weight[:, :, :, 3:split_at]
    weight_rand = attention_weight[:, :, :, split_at:]
    mixed = product("hiajb,ijbhd->iahd", weight_win, window[1])
    mixed = mixed + product("hiajb,jbhd->iahd", weight_glob, global_pair[1])
    mixed = mixed + product("hiajb,hijbd->iahd", weight_rand, rand_values)
    attended = mixed.astype(jnp.bfloat16)
    out_rows = attended.reshape(tokens_here, width_here)
    row_delta = jnp.sum(
        incoming_gradient.astype(jnp.float32) * attended.astype(jnp.float32), axis=3
    ).transpose(2, 0, 1)[:, :, :, None, None]
    probability_gradient = jnp.concatenate(
        [
            product("iahd,ijbhd->hiajb", incoming_gradient, window[1]),
            product("iahd,jbhd->hiajb", incoming_gradient, global_pair[1]),
            product("iahd,hijbd->hiajb", incoming_gradient, rand_values),
        ],
        axis=3,
    )
    logit_gradient = (probability * (probability_gradient - row_delta)).astype(jnp.bfloat16)
    grad_win = logit_gradient[:, :, :, :3]
    grad_glob = logit_gradient[:, :, :, 3:split_at]
    grad_rand = logit_gradient[:, :, :, split_at:]
    query_gradient = product("hiajb,ijbhd->iahd", grad_win, window[0])
    query_gradient = query_gradient + product("hiajb,jbhd->iahd", grad_glob, global_pair[0])
    query_gradient = query_gradient + product("hiajb,hijbd->iahd", grad_rand, rand_keys)
    query_gradient = (
        (score_scale * query_gradient).astype(jnp.bfloat16).reshape(tokens_here, width_here)
    )
    near_grads = jnp.stack(
        [
            score_scale * product("hiajb,iahd->ijbhd", grad_win, query_tiles),
            product("hiajb,iahd->ijbhd", weight_win, incoming_gradient),
        ]
    )
    accum = (
        spread(near_grads[:, :, 1], 1)
        + spread(near_grads[:, :, 0], 0)
        + spread(near_grads[:, :, 2], 2)
    )
    rim_rows = jnp.concatenate([accum[:, :1], accum[:, -1:]], axis=1).reshape(
        2, 2 * BLOCK, width_here
    )
    arrived = extended(rim_rows.astype(jnp.bfloat16), (("seq", 1),), BLOCK).astype(rim_rows.dtype)
    arrived = arrived.reshape(2, 4, BLOCK, heads_here, HEAD_DIM)
    own_blocks = accum[:, 1:-1]
    own_blocks = own_blocks.at[:, 0].add(arrived[:, 0]).at[:, -1].add(arrived[:, 3])
    far_keys = score_scale * product("hiajb,iahd->jbhd", grad_glob, query_tiles)
    far_values = product("hiajb,iahd->jbhd", weight_glob, incoming_gradient)
    sum_keys, sum_values = lax.psum((far_keys, far_values), "seq")
    for glob_index in range(GLOB_BLOCKS):
        target = global_blocks[glob_index]
        owner_flag = (target // blocks_here == my_shard).astype(jnp.float32)
        addition = jnp.stack([sum_keys[glob_index], sum_values[glob_index]]) * owner_flag
        own_blocks = own_blocks.at[:, target % blocks_here].add(addition)
    tile_zero = jnp.zeros((shards, slot_count, BLOCK, HEAD_DIM), jnp.bfloat16)
    rand_grad_keys = (
        (score_scale * product("hiajb,iahd->hijbd", grad_rand, query_tiles))
        .astype(jnp.bfloat16)
        .reshape(requests, BLOCK, HEAD_DIM)
    )
    rand_grad_values = (
        product("hiajb,iahd->hijbd", weight_rand, incoming_gradient)
        .astype(jnp.bfloat16)
        .reshape(requests, BLOCK, HEAD_DIM)
    )
    keys_box = tile_zero.at[my_owner, my_slot].set(rand_grad_keys)
    values_box = tile_zero.at[my_owner, my_slot].set(rand_grad_values)
    back_keys, back_values = (
        lax.all_to_all(keys_box, "seq", split_axis=0, concat_axis=0, tiled=True),
        lax.all_to_all(values_box, "seq", split_axis=0, concat_axis=0, tiled=True),
    )
    selector = (
        (
            send_ids[:, :, None]
            == jnp.arange(heads_here * blocks_here, dtype=jnp.int32)[None, None, :]
        )
        & slot_used[:, :, None]
    ).astype(jnp.bfloat16)

    def collect(returned):
        summed = product("ncs,ncbd->sbd", selector, returned)
        return summed.reshape(heads_here, blocks_here, BLOCK, HEAD_DIM).transpose(1, 2, 0, 3)

    grad_key = (
        (own_blocks[0] + collect(back_keys)).astype(jnp.bfloat16).reshape(tokens_here, width_here)
    )
    grad_value = (
        (own_blocks[1] + collect(back_values)).astype(jnp.bfloat16).reshape(tokens_here, width_here)
    )
    return (
        lax.all_to_all(out_rows, "head", split_axis=0, concat_axis=1, tiled=True),
        lax.all_to_all(query_gradient, "head", split_axis=0, concat_axis=1, tiled=True),
        lax.all_to_all(grad_key, "head", split_axis=0, concat_axis=1, tiled=True),
        lax.all_to_all(grad_value, "head", split_axis=0, concat_axis=1, tiled=True),
    )


def solution(mesh):
    placed = (
        P(("seq", "head"), None),
        P(("seq", "head"), None),
        P(("seq", "head"), None),
        P(("seq", "head"), None),
        P(),
        P(),
    )
    return jax.shard_map(
        body,
        mesh=mesh,
        in_specs=placed,
        out_specs=(
            P(("seq", "head"), None),
            P(("seq", "head"), None),
            P(("seq", "head"), None),
            P(("seq", "head"), None),
        ),
        check_vma=False,
    )
```

profile of v0, /device:TPU:1, one launch (start us, length us, event | category | flops | bytes accessed | tf_op | source)
XLA Modules:
  0.0 357.0 jit_solution(5172477424178291853)
XLA Ops:
  8.9 4.3 %all-to-all-start.6 = ((bf16[32,4,1024]{2,0,1:T(8,128)(2,1)}), bf16[32,4,1024]{2,0,1:T(8,128)(2,1)S(1)}, u32[]{:S(2)}, u32[]{:S(2)}) async-start(bf16[32,4,1024]{2,0,1:T(8,128)(2,1)} %bitcast.322), calls=%async_computation.6 | async-start | bytes 524288 | tf_op jit(solution)/shard_map/all_to_all | solution.py:45
  29.1 5.0 %all-to-all-done.1 = bf16[32,4,1024]{2,0,1:T(8,128)(2,1)S(1)} async-done(((bf16[32,4,1024]{2,0,1:T(8,128)(2,1)}), bf16[32,4,1024]{2,0,1:T(8,128)(2,1)S(1)}, u32[]{:S(2)}, u32[]{:S(2)}) %all-to-all-start.1) | async-done | bytes 262176 | tf_op jit(solution)/shard_map/all_to_all | solution.py:44
  34.1 4.4 %all-to-all-start = ((bf16[32,4,1024]{2,0,1:T(8,128)(2,1)}), bf16[32,4,1024]{2,0,1:T(8,128)(2,1)S(1)}, u32[]{:S(2)}, u32[]{:S(2)}) async-start(bf16[32,4,1024]{2,0,1:T(8,128)(2,1)} %bitcast.325), calls=%async_computation | async-start | bytes 524288 | tf_op jit(solution)/shard_map/all_to_all | solution.py:43
  38.7 4.9 %all-to-all-done = bf16[32,4,1024]{2,0,1:T(8,128)(2,1)S(1)} async-done(((bf16[32,4,1024]{2,0,1:T(8,128)(2,1)}), bf16[32,4,1024]{2,0,1:T(8,128)(2,1)S(1)}, u32[]{:S(2)}, u32[]{:S(2)}) %all-to-all-start) | async-done | bytes 262176 | tf_op jit(solution)/shard_map/all_to_all | solution.py:43
  43.6 4.9 %all-to-all-start.2 = ((bf16[32,4,1024]{2,0,1:T(8,128)(2,1)}), bf16[32,4,1024]{2,0,1:T(8,128)(2,1)}, u32[]{:S(2)}, u32[]{:S(2)}) async-start(bf16[32,4,1024]{2,0,1:T(8,128)(2,1)} %bitcast.323), calls=%async_computation.2 | async-start | bytes 524288 | tf_op jit(solution)/shard_map/all_to_all | solution.py:42
  53.8 6.3 %all-to-all-start.3 = ((bf16[8,7,64,128]{3,2,1,0:T(8,128)(2,1)}), bf16[8,7,64,128]{3,2,1,0:T(8,128)(2,1)S(1)}, u32[]{:S(2)}, u32[]{:S(2)}) async-start(bf16[8,7,64,128]{3,2,1,0:T(8,128)(2,1)} %get-tuple-element.93), calls=%async_computation.3 | async-start | bytes 1835008 | tf_op jit(solution)/shard_map/all_to_all | solution.py:97
  63.9 4.7 %collective-permute-start = (bf16[2,64,1024]{2,1,0:T(8,128)(2,1)S(1)}, bf16[2,64,1024]{2,1,0:T(8,128)(2,1)}, u32[]{:S(2)}, u32[]{:S(2)}) collective-permute-start(bf16[2,64,1024]{2,1,0:T(8,128)(2,1)S(1)} %get-tuple-element.86), channel_id=1, source_target_pairs={{0,4},{4,8},{8,12},{12,16},{16,20},{20,24},{24,28},{1,5},{5,9},{9,... | collective-permute-start | bytes 786440 | tf_op jit(solution)/shard_map/ppermute | solution.py:19
  69.6 7.6 %collective-permute-done.1 = bf16[2,64,1024]{2,1,0:T(8,128)(2,1)} collective-permute-done((bf16[2,64,1024]{2,1,0:T(8,128)(2,1)}, bf16[2,64,1024]{2,1,0:T(8,128)(2,1)}, u32[]{:S(2)}, u32[]{:S(2)}) %collective-permute-start.1) | collective-permute-done | bytes 262176 | tf_op jit(solution)/shard_map/ppermute | solution.py:20
  77.2 6.3 %collective-permute-done = bf16[2,64,1024]{2,1,0:T(8,128)(2,1)} collective-permute-done((bf16[2,64,1024]{2,1,0:T(8,128)(2,1)S(1)}, bf16[2,64,1024]{2,1,0:T(8,128)(2,1)}, u32[]{:S(2)}, u32[]{:S(2)}) %collective-permute-start) | collective-permute-done | bytes 262176 | tf_op jit(solution)/shard_map/ppermute | solution.py:19
  88.9 56.2 %all-reduce.10.cloned.1.call-done = (bf16[2,1,64,8,128]{4,2,1,3,0:T(8,128)(2,1)}, bf16[2,1,64,8,128]{4,2,1,3,0:T(8,128)(2,1)}) async-done(((bf16[2,1,64,8,128]{4,2,1,3,0:T(8,128)(2,1)}, bf16[2,1,64,8,128]{4,2,1,3,0:T(8,128)(2,1)}), (bf16[2,1,64,8,128]{4,2,1,3,0:T(8,128)(2,1)}, bf16[2,1,64,8,128]{4,2,1,3,0:T(8,128)(2,1)})) %all-reduce.10.cloned.1.call-update) | async-done | bytes 524304 | tf_op jit(solution)/shard_map/psum | solution.py:27
  149.9 4.4 %all-to-all-start.4 = ((bf16[8,7,64,128]{3,2,1,0:T(8,128)(2,1)}), bf16[8,7,64,128]{3,2,1,0:T(8,128)(2,1)}, u32[]{:S(2)}, u32[]{:S(2)}) async-start(bf16[8,7,64,128]{3,2,1,0:T(8,128)(2,1)} %get-tuple-element.92), calls=%async_computation.4 | async-start | bytes 1835008 | tf_op jit(solution)/shard_map/all_to_all | solution.py:98
  164.0 11.1 %all-to-all-done.4 = bf16[8,7,64,128]{3,2,1,0:T(8,128)(2,1)} async-done(((bf16[8,7,64,128]{3,2,1,0:T(8,128)(2,1)}), bf16[8,7,64,128]{3,2,1,0:T(8,128)(2,1)}, u32[]{:S(2)}, u32[]{:S(2)}) %all-to-all-start.4) | async-done | bytes 917536 | tf_op jit(solution)/shard_map/all_to_all | solution.py:98
  191.9 6.8 %scatter_fusion.1 = bf16[8,7,64,128]{3,2,1,0:T(8,128)(2,1)} fusion(bf16[8,7,64,128]{3,2,1,0:T(8,128)(2,1)} %broadcast_in_dim.44.clone, s32[48]{0:T(128)S(1)} %get-tuple-element.90, bf16[48,64,128]{2,1,0:T(8,128)(2,1)S(1)} %bitcast.344), kind=kCustom, calls=%fused_computation.5 | custom fusion | bytes 2359680 | tf_op jit(solution)/shard_map/scatter | solution.py:195
  198.7 5.7 %all-to-all-start.10 = ((bf16[8,7,64,128]{3,2,1,0:T(8,128)(2,1)}), bf16[8,7,64,128]{3,2,1,0:T(8,128)(2,1)}, u32[]{:S(2)}, u32[]{:S(2)}) async-start(bf16[8,7,64,128]{3,2,1,0:T(8,128)(2,1)} %scatter_fusion.1), calls=%async_computation.10 | async-start | bytes 1835008 | tf_op jit(solution)/shard_map/all_to_all | solution.py:198
  206.7 4.7 %collective-permute-start.2 = (bf16[2,64,1024]{2,1,0:T(8,128)(2,1)}, bf16[2,64,1024]{2,1,0:T(8,128)(2,1)}, u32[]{:S(2)}, u32[]{:S(2)}) collective-permute-start(bf16[2,64,1024]{2,1,0:T(8,128)(2,1)} %get-tuple-element.84), channel_id=1, source_target_pairs={{0,4},{4,8},{8,12},{12,16},{16,20},{20,24},{24,28},{1,5},{5,9},{9,... | collective-permute-start | bytes 786440 | tf_op jit(solution)/shard_map/ppermute | solution.py:19
  222.7 7.6 %scatter_fusion = bf16[8,7,64,128]{3,2,1,0:T(8,128)(2,1)} fusion(bf16[8,7,64,128]{3,2,1,0:T(8,128)(2,1)} %broadcast_in_dim.44.clone.1, s32[48]{0:T(128)S(1)} %get-tuple-element.90, bf16[48,64,128]{2,1,0:T(8,128)(2,1)} %bitcast.345), kind=kCustom, calls=%fused_computation.4 | custom fusion | bytes 2359680 | tf_op jit(solution)/shard_map/scatter | solution.py:194
  233.6 17.1 %all-to-all-start.8 = ((bf16[8,7,64,128]{3,2,1,0:T(8,128)(2,1)}), bf16[8,7,64,128]{3,2,1,0:T(8,128)(2,1)}, u32[]{:S(2)}, u32[]{:S(2)}) async-start(bf16[8,7,64,128]{3,2,1,0:T(8,128)(2,1)} %scatter_fusion), calls=%async_computation.8 | async-start | bytes 1835008 | tf_op jit(solution)/shard_map/all_to_all | solution.py:197
  252.3 53.6 %all-reduce.8.cloned.1.call-done = (f32[2,64,8,128]{3,1,2,0:T(8,128)}, f32[2,64,8,128]{3,1,2,0:T(8,128)}) async-done(((f32[2,64,8,128]{3,1,2,0:T(8,128)}, f32[2,64,8,128]{3,1,2,0:T(8,128)}), (f32[2,64,8,128]{3,1,2,0:T(8,128)}, f32[2,64,8,128]{3,1,2,0:T(8,128)})) %all-reduce.8.cloned.1.call-update) | async-done | bytes 1048592 | tf_op jit(solution)/shard_map/psum | solution.py:177
  311.3 4.7 %all-to-all-start.5 = ((bf16[4,32,1024]{2,1,0:T(8,128)(2,1)}), bf16[4,32,1024]{2,1,0:T(8,128)(2,1)S(1)}, u32[]{:S(2)}, u32[]{:S(2)}) async-start(bf16[4,32,1024]{2,1,0:T(8,128)(2,1)} %all_to_all.127), calls=%async_computation.5 | async-start | bytes 524288 | tf_op jit(solution)/shard_map/all_to_all | solution.py:219
  321.2 4.2 %all-to-all-start.7 = ((bf16[4,32,1024]{2,1,0:T(8,128)(2,1)}), bf16[4,32,1024]{2,1,0:T(8,128)(2,1)S(1)}, u32[]{:S(2)}, u32[]{:S(2)}) async-start(bf16[4,32,1024]{2,1,0:T(8,128)(2,1)} %all_to_all.134), calls=%async_computation.7 | async-start | bytes 524288 | tf_op jit(solution)/shard_map/all_to_all | solution.py:220
  326.9 3.8 %all-to-all-done.7 = bf16[4,32,1024]{2,1,0:T(8,128)(2,1)S(1)} async-done(((bf16[4,32,1024]{2,1,0:T(8,128)(2,1)}), bf16[4,32,1024]{2,1,0:T(8,128)(2,1)S(1)}, u32[]{:S(2)}, u32[]{:S(2)}) %all-to-all-start.7) | async-done | bytes 262176 | tf_op jit(solution)/shard_map/all_to_all | solution.py:220
  330.6 4.2 %all-to-all-start.9 = ((bf16[4,32,1024]{2,1,0:T(8,128)(2,1)}), bf16[4,32,1024]{2,1,0:T(8,128)(2,1)S(1)}, u32[]{:S(2)}, u32[]{:S(2)}) async-start(bf16[4,32,1024]{2,1,0:T(8,128)(2,1)} %all_to_all.139), calls=%async_computation.9 | async-start | bytes 524288 | tf_op jit(solution)/shard_map/all_to_all | solution.py:221
  335.9 4.2 %all-to-all-done.9 = bf16[4,32,1024]{2,1,0:T(8,128)(2,1)S(1)} async-done(((bf16[4,32,1024]{2,1,0:T(8,128)(2,1)}), bf16[4,32,1024]{2,1,0:T(8,128)(2,1)S(1)}, u32[]{:S(2)}, u32[]{:S(2)}) %all-to-all-start.9) | async-done | bytes 262176 | tf_op jit(solution)/shard_map/all_to_all | solution.py:221
  340.1 4.2 %all-to-all-start.11 = ((bf16[4,32,1024]{2,1,0:T(8,128)(2,1)}), bf16[4,32,1024]{2,1,0:T(8,128)(2,1)S(1)}, u32[]{:S(2)}, u32[]{:S(2)}) async-start(bf16[4,32,1024]{2,1,0:T(8,128)(2,1)} %all_to_all.144), calls=%async_computation.11 | async-start | bytes 524288 | tf_op jit(solution)/shard_map/all_to_all | solution.py:222
  (210 shorter events, 95.8 us)
Async XLA Ops:
  7.2 17.6 %copy-start.37 = (s32[5]{0:T(128)S(1)}, s32[5]{0:T(128)}, u32[]{:S(2)}) copy-start(s32[5]{0:T(128)} %constant.248.clone.1) | copy-start | bytes 64
  7.2 16.6 %copy-start.36 = (bf16[32,4096]{1,0:T(8,128)(2,1)S(1)}, bf16[32,4096]{1,0:T(8,128)(2,1)}, u32[]{:S(2)}) copy-start(bf16[32,4096]{1,0:T(8,128)(2,1)} %param.14) | copy-start | bytes 786436
  8.9 16.7 %all-to-all-start.6 = ((bf16[32,4,1024]{2,0,1:T(8,128)(2,1)}), bf16[32,4,1024]{2,0,1:T(8,128)(2,1)S(1)}, u32[]{:S(2)}, u32[]{:S(2)}) async-start(bf16[32,4,1024]{2,0,1:T(8,128)(2,1)} %bitcast.322), calls=%async_computation.6 | async-start | bytes 524288 | tf_op jit(solution)/shard_map/all_to_all | solution.py:45
  25.6 8.5 %all-to-all-start.1 = ((bf16[32,4,1024]{2,0,1:T(8,128)(2,1)}), bf16[32,4,1024]{2,0,1:T(8,128)(2,1)S(1)}, u32[]{:S(2)}, u32[]{:S(2)}) async-start(bf16[32,4,1024]{2,0,1:T(8,128)(2,1)} %bitcast.324), calls=%async_computation.1 | async-start | bytes 524288 | tf_op jit(solution)/shard_map/all_to_all | solution.py:44
  34.1 9.5 %all-to-all-start = ((bf16[32,4,1024]{2,0,1:T(8,128)(2,1)}), bf16[32,4,1024]{2,0,1:T(8,128)(2,1)S(1)}, u32[]{:S(2)}, u32[]{:S(2)}) async-start(bf16[32,4,1024]{2,0,1:T(8,128)(2,1)} %bitcast.325), calls=%async_computation | async-start | bytes 524288 | tf_op jit(solution)/shard_map/all_to_all | solution.py:43
  38.6 30.9 %copy-start.26 = (bf16[16,8,8,128]{3,2,1,0:T(8,128)(2,1)}, bf16[16,8,8,128]{3,2,1,0:T(8,128)(2,1)S(1)}, u32[]{:S(2)}) copy-start(bf16[16,8,8,128]{3,2,1,0:T(8,128)(2,1)S(1)} %copy.460) | copy-start | bytes 786436
  43.6 10.2 %all-to-all-start.2 = ((bf16[32,4,1024]{2,0,1:T(8,128)(2,1)}), bf16[32,4,1024]{2,0,1:T(8,128)(2,1)}, u32[]{:S(2)}, u32[]{:S(2)}) async-start(bf16[32,4,1024]{2,0,1:T(8,128)(2,1)} %bitcast.323), calls=%async_computation.2 | async-start | bytes 524288 | tf_op jit(solution)/shard_map/all_to_all | solution.py:42
  53.8 96.1 %all-to-all-start.3 = ((bf16[8,7,64,128]{3,2,1,0:T(8,128)(2,1)}), bf16[8,7,64,128]{3,2,1,0:T(8,128)(2,1)S(1)}, u32[]{:S(2)}, u32[]{:S(2)}) async-start(bf16[8,7,64,128]{3,2,1,0:T(8,128)(2,1)} %get-tuple-element.93), calls=%async_computation.3 | async-start | bytes 1835008 | tf_op jit(solution)/shard_map/all_to_all | solution.py:97
  60.1 85.1 %all-reduce.10.cloned.1.call-start = ((), (), s32[]{:S(2)}) async-start(), calls=%async_computation.13 | async-start | bytes 1048576 | tf_op jit(solution)/shard_map/psum | solution.py:27
  62.6 14.6 %collective-permute-start.1 = (bf16[2,64,1024]{2,1,0:T(8,128)(2,1)}, bf16[2,64,1024]{2,1,0:T(8,128)(2,1)}, u32[]{:S(2)}, u32[]{:S(2)}) collective-permute-start(bf16[2,64,1024]{2,1,0:T(8,128)(2,1)} %get-tuple-element.87), channel_id=1, source_target_pairs={{4,0},{8,4},{12,8},{16,12},{20,16},{24,20},{28,24},{5,1},{9,5},{13... | collective-permute-start | bytes 786440 | tf_op jit(solution)/shard_map/ppermute | solution.py:20
  63.9 19.6 %collective-permute-start = (bf16[2,64,1024]{2,1,0:T(8,128)(2,1)S(1)}, bf16[2,64,1024]{2,1,0:T(8,128)(2,1)}, u32[]{:S(2)}, u32[]{:S(2)}) collective-permute-start(bf16[2,64,1024]{2,1,0:T(8,128)(2,1)S(1)} %get-tuple-element.86), channel_id=1, source_target_pairs={{0,4},{4,8},{8,12},{12,16},{16,20},{20,24},{24,28},{1,5},{5,9},{9,... | collective-permute-start | bytes 786440 | tf_op jit(solution)/shard_map/ppermute | solution.py:19
  69.6 78.9 %copy-start.7 = (bf16[2,64,8,128,1]{3,2,1,0,4:T(8,128)(2,1)}, bf16[2,64,8,128,1]{3,2,1,0,4:T(8,128)(2,1)S(1)}, u32[]{:S(2)}) copy-start(bf16[2,64,8,128,1]{3,2,1,0,4:T(8,128)(2,1)S(1)} %bitcast_bitcast_fusion) | copy-start | bytes 786436
  149.9 25.2 %all-to-all-start.4 = ((bf16[8,7,64,128]{3,2,1,0:T(8,128)(2,1)}), bf16[8,7,64,128]{3,2,1,0:T(8,128)(2,1)}, u32[]{:S(2)}, u32[]{:S(2)}) async-start(bf16[8,7,64,128]{3,2,1,0:T(8,128)(2,1)} %get-tuple-element.92), calls=%async_computation.4 | async-start | bytes 1835008 | tf_op jit(solution)/shard_map/all_to_all | solution.py:98
  191.8 19.6 %copy-start.28 = (bf16[16,8,8,128]{3,2,1,0:T(8,128)(2,1)S(1)}, bf16[16,8,8,128]{3,2,1,0:T(8,128)(2,1)}, u32[]{:S(2)}) copy-start(bf16[16,8,8,128]{3,2,1,0:T(8,128)(2,1)} %copy-done.26) | copy-start | bytes 786436
  198.7 34.9 %all-to-all-start.10 = ((bf16[8,7,64,128]{3,2,1,0:T(8,128)(2,1)}), bf16[8,7,64,128]{3,2,1,0:T(8,128)(2,1)}, u32[]{:S(2)}, u32[]{:S(2)}) async-start(bf16[8,7,64,128]{3,2,1,0:T(8,128)(2,1)} %scatter_fusion.1), calls=%async_computation.10 | async-start | bytes 1835008 | tf_op jit(solution)/shard_map/all_to_all | solution.py:198
  204.4 101.5 %all-reduce.8.cloned.1.call-start = ((), (), s32[]{:S(2)}) async-start(), calls=%async_computation.12 | async-start | bytes 2097152 | tf_op jit(solution)/shard_map/psum | solution.py:177
  205.3 25.0 %collective-permute-start.3 = (bf16[2,64,1024]{2,1,0:T(8,128)(2,1)}, bf16[2,64,1024]{2,1,0:T(8,128)(2,1)}, u32[]{:S(2)}, u32[]{:S(2)}) collective-permute-start(bf16[2,64,1024]{2,1,0:T(8,128)(2,1)} %get-tuple-element.85), channel_id=1, source_target_pairs={{4,0},{8,4},{12,8},{16,12},{20,16},{24,20},{28,24},{5,1},{9,5},{13... | collective-permute-start | bytes 786440 | tf_op jit(solution)/shard_map/ppermute | solution.py:20
  206.7 23.6 %collective-permute-start.2 = (bf16[2,64,1024]{2,1,0:T(8,128)(2,1)}, bf16[2,64,1024]{2,1,0:T(8,128)(2,1)}, u32[]{:S(2)}, u32[]{:S(2)}) collective-permute-start(bf16[2,64,1024]{2,1,0:T(8,128)(2,1)} %get-tuple-element.84), channel_id=1, source_target_pairs={{0,4},{4,8},{8,12},{12,16},{16,20},{20,24},{24,28},{1,5},{5,9},{9,... | collective-permute-start | bytes 786440 | tf_op jit(solution)/shard_map/ppermute | solution.py:19
  233.6 77.7 %all-to-all-start.8 = ((bf16[8,7,64,128]{3,2,1,0:T(8,128)(2,1)}), bf16[8,7,64,128]{3,2,1,0:T(8,128)(2,1)}, u32[]{:S(2)}, u32[]{:S(2)}) async-start(bf16[8,7,64,128]{3,2,1,0:T(8,128)(2,1)} %scatter_fusion), calls=%async_computation.8 | async-start | bytes 1835008 | tf_op jit(solution)/shard_map/all_to_all | solution.py:197
  311.3 9.9 %all-to-all-start.5 = ((bf16[4,32,1024]{2,1,0:T(8,128)(2,1)}), bf16[4,32,1024]{2,1,0:T(8,128)(2,1)S(1)}, u32[]{:S(2)}, u32[]{:S(2)}) async-start(bf16[4,32,1024]{2,1,0:T(8,128)(2,1)} %all_to_all.127), calls=%async_computation.5 | async-start | bytes 524288 | tf_op jit(solution)/shard_map/all_to_all | solution.py:219
  321.2 9.4 %all-to-all-start.7 = ((bf16[4,32,1024]{2,1,0:T(8,128)(2,1)}), bf16[4,32,1024]{2,1,0:T(8,128)(2,1)S(1)}, u32[]{:S(2)}, u32[]{:S(2)}) async-start(bf16[4,32,1024]{2,1,0:T(8,128)(2,1)} %all_to_all.134), calls=%async_computation.7 | async-start | bytes 524288 | tf_op jit(solution)/shard_map/all_to_all | solution.py:220
  326.0 24.2 %copy-start.1 = (s32[32,16,3]{0,1,2:T(8,128)S(1)}, s32[32,16,3]{0,1,2:T(8,128)}, u32[]{:S(2)}) copy-start(s32[32,16,3]{0,1,2:T(8,128)} %param.18) | copy-start | bytes 18436
  330.6 9.4 %all-to-all-start.9 = ((bf16[4,32,1024]{2,1,0:T(8,128)(2,1)}), bf16[4,32,1024]{2,1,0:T(8,128)(2,1)S(1)}, u32[]{:S(2)}, u32[]{:S(2)}) async-start(bf16[4,32,1024]{2,1,0:T(8,128)(2,1)} %all_to_all.139), calls=%async_computation.9 | async-start | bytes 524288 | tf_op jit(solution)/shard_map/all_to_all | solution.py:221
  340.1 9.4 %all-to-all-start.11 = ((bf16[4,32,1024]{2,1,0:T(8,128)(2,1)}), bf16[4,32,1024]{2,1,0:T(8,128)(2,1)S(1)}, u32[]{:S(2)}, u32[]{:S(2)}) async-start(bf16[4,32,1024]{2,1,0:T(8,128)(2,1)} %all_to_all.144), calls=%async_computation.11 | async-start | bytes 524288 | tf_op jit(solution)/shard_map/all_to_all | solution.py:222
  (32 other events, 144.0 us)
Sparse Core Ops, SparseCore 0:
  69.7 75.4 all-reduce.9
  215.7 90.1 all-reduce.7
where the time goes:
time: 360 us; the launch traced here: 357 us
  waiting for transfers between devices  160 us (44%)
  starting transfers between devices  80.1 us (22%)
  local copies, waits for them, and re-layouts  54.9 us (15%)
  matrix products  24.8 us (7%)
  between operations  20.1 us (6%)
  other arithmetic  16.7 us (5%)
    psum x1, waiting for transfers between devices, spread_2(): return lax.psum(jnp.where(mine, shard, jnp.zeros_like(shard)), axis)  56.2 us
    psum x1, waiting for transfers between devices, body(): sum_keys, sum_values = lax.psum((far_keys, far_values), 'seq')  53.6 us
    dot_general x20, matrix products, product(): jnp.einsum(formula, former, latter, preferred_element_type=jnp.float32)  24.8 us
    all_to_all x1, starting transfers between devices, body(): lax.all_to_all(keys_box, 'seq', split_axis=0, concat_axis=0, tiled=True)  17.1 us
    all_to_all x1, waiting for transfers between devices, body(): lax.all_to_all(value_send, 'seq', split_axis=0, concat_axis=0, tiled=True)  11.1 us
    ppermute x2, starting transfers between devices, extended(): before = lax.ppermute(last, axis, up)  9.41 us
    scatter x1, local copies, waits for them, and re-layouts, body(): keys_box = tile_zero.at[my_owner, my_slot].set(rand_grad_keys)  7.63 us
    ppermute x2, waiting for transfers between devices, extended(): after = lax.ppermute(first, axis, down)  7.58 us
  transfers between devices with their start and end apart: 18, of which 12 were waited for; matrix products, arithmetic and copies ran while one was open for 18% of the time, Pallas kernels for 0%

commit v1 on v0

v1 whole, which is shorter than its diff:
```python
import functools
import math

import jax
import jax.numpy as jnp
from jax import lax
from jax.experimental import pallas as pl
from jax.experimental.pallas import tpu as pltpu
from jax.sharding import Mesh
from jax.sharding import PartitionSpec as P

HEAD_DIM = 128
BLOCK = 64
SCALE = HEAD_DIM**-0.5
QUERY_TILE = 256
KEY_TILE = 512

WHOLE = pl.BlockSpec(memory_space=pltpu.VMEM)
FAR = pl.BlockSpec(memory_space=pltpu.HBM)


def dot(a, b):
    return lax.dot_general(a, b, (((1,), (0,)), ((), ())), preferred_element_type=jnp.float32)


def dot_nt(a, b):
    return lax.dot_general(a, b, (((1,), (1,)), ((), ())), preferred_element_type=jnp.float32)


def each(count, step, start):
    if count <= 4:
        carry = start
        for i in range(count):
            carry = step(i, carry)
        return carry
    return lax.fori_loop(0, count, step, start)


def copies(pairs, sems):
    made = [pltpu.make_async_copy(a, b, sems.at[i]) for i, (a, b) in enumerate(pairs)]
    for copy in made:
        copy.start()
    return made


def wait_all(made):
    for copy in made:
        copy.wait()


def pack_kernel(random_ref, global_ref, *refs):
    *ins, out, random_out, global_out, held, sems = refs
    pairs = [(x, held.at[a]) for a, x in enumerate(ins)]
    pairs += [(random_ref, random_out), (global_ref, global_out)]
    wait_all(copies(pairs, sems))
    for h in range(out.shape[0]):
        for a in range(len(ins)):
            out[h, a] = held[a, :, h * HEAD_DIM : (h + 1) * HEAD_DIM]


def pack(arrays, tables):
    rows, width = arrays[0].shape
    kind = arrays[0].dtype
    shape = (width // HEAD_DIM, len(arrays), rows, HEAD_DIM)
    ins = [pltpu.with_memory_space_constraint(x, pltpu.HBM) for x in tables + arrays]
    return pl.pallas_call(
        pack_kernel,
        out_shape=[pltpu.VMEM(shape, kind)] + [pltpu.VMEM(x.shape, x.dtype) for x in tables],
        in_specs=[FAR] * len(ins),
        out_specs=[WHOLE] * (1 + len(tables)),
        scratch_shapes=[
            pltpu.VMEM((len(arrays), rows, width), kind),
            pltpu.SemaphoreType.DMA((len(ins),)),
        ],
        compiler_params=pltpu.CompilerParams(vmem_limit_bytes=8 << 20),
    )(*ins)


def unpack_kernel(packed, *refs):
    outs, (held, sems) = refs[:-2], refs[-2:]
    leaving = []
    for a, out in enumerate(outs):
        for h in range(packed.shape[0]):
            held[a, :, h * HEAD_DIM : (h + 1) * HEAD_DIM] = packed[h, a]
        leaving.append(pltpu.make_async_copy(held.at[a], out, sems.at[a]))
        leaving[-1].start()
    wait_all(leaving)


def unpack(packed):
    heads, arrays, rows, depth = packed.shape
    return pl.pallas_call(
        unpack_kernel,
        out_shape=[jax.ShapeDtypeStruct((rows, heads * depth), packed.dtype)] * arrays,
        in_specs=[WHOLE],
        out_specs=[FAR] * arrays,
        scratch_shapes=[
            pltpu.VMEM((arrays, rows, heads * depth), packed.dtype),
            pltpu.SemaphoreType.DMA((arrays,)),
        ],
        compiler_params=pltpu.CompilerParams(vmem_limit_bytes=8 << 20),
    )(packed)


def tile_of(pair, start, size):
    ref, slot = pair
    rows = ref.shape[2]
    lanes = pl.ds(start // rows, size // rows)
    return ref[lanes, slot].reshape(size, HEAD_DIM)


def put(pair, start, tile):
    ref, slot = pair
    size, rows = tile.shape[0], ref.shape[2]
    lanes = pl.ds(start // rows, size // rows)
    ref[lanes, slot] = tile.astype(ref.dtype).reshape(size // rows, rows, HEAD_DIM)


def span(i, size):
    return pl.ds(pl.multiple_of(i * size, size), size)


def flip(pair, out, length):
    step = min(512, length)

    def one(i, _):
        tile = tile_of(pair, i * step, step)
        out[:HEAD_DIM, span(i, step)] = tile.astype(jnp.float32).T.astype(out.dtype)
        return 0

    each(length // step, one, 0)


def list_bias(random_ref, global_ref, bias_ref):
    steps, group, queries = bias_ref.shape
    blocks, total = queries // BLOCK, steps * group
    first = lax.axis_index("crew") * blocks
    shape = (blocks, total)
    names = lax.broadcasted_iota(jnp.int32, shape, 1)
    own = first + lax.broadcasted_iota(jnp.int32, shape, 0)
    times = (jnp.abs(names - own) <= 1).astype(jnp.float32)
    for i in range(global_ref.shape[1]):
        times += (names == global_ref[:, i : i + 1]).astype(jnp.float32)
    heads = random_ref.shape[2]
    mine = lax.broadcasted_iota(jnp.int32, (blocks, heads), 1) == lax.axis_index("lane")
    for i in range(random_ref.shape[0]):
        picks = jnp.where(mine, random_ref[i, pl.ds(first, blocks), :], 0)
        times += (names == jnp.sum(picks, axis=1, keepdims=True)).astype(jnp.float32)
    place = lax.broadcasted_iota(jnp.int32, (blocks, queries), 1) // BLOCK
    place = (place == lax.broadcasted_iota(jnp.int32, (blocks, queries), 0)).astype(jnp.bfloat16)
    wide = lax.dot_general(
        times.astype(jnp.bfloat16), place, (((0,), (0,)), ((), ())), preferred_element_type=jnp.float32
    )
    bias = jnp.where(wide > 0.0, jnp.log2(jnp.maximum(wide, 1.0)), -jnp.inf)
    bias_ref[...] = bias.reshape(steps, group, queries)


def attend_kernel(
    q_at, g_at, k_at, v_at, random_ref, global_ref, out_at, dq_at, dk_at, dv_at,
    score_ref, w_ref, ds_ref, bias_ref, kt_ref, vt_ref, gt_ref, gs_ref, delta_ref,
):
    keys, queries = w_ref.shape
    steps = keys // KEY_TILE
    turns = queries // QUERY_TILE
    factor = SCALE * math.log2(math.e)
    list_bias(random_ref, global_ref, bias_ref)
    flip(v_at, vt_ref, keys)
    vt_ref[HEAD_DIM:, :] = jnp.ones_like(vt_ref[HEAD_DIM:, :])

    def through(left_ref, right_ref, here):
        def add(c, total):
            at = span(c, KEY_TILE)
            return total + dot(left_ref[:, at], right_ref[at, here])

        if steps <= 4:
            return dot(left_ref[...], right_ref[:, here])
        return each(steps, add, jnp.zeros((left_ref.shape[0], QUERY_TILE), jnp.float32))

    def blocks_of(x):
        return x.reshape(KEY_TILE // BLOCK, BLOCK, QUERY_TILE)

    def score(t):
        here = span(t, QUERY_TILE)
        held = score_ref.at[t % 2]
        q = tile_of(q_at, t * QUERY_TILE, QUERY_TILE)

        def one(c, top):
            raw = dot_nt(tile_of(k_at, c * KEY_TILE, KEY_TILE), q)
            held[span(c, KEY_TILE), :] = raw
            listed = jnp.where(bias_ref[c, :, here] > -jnp.inf, 0.0, -jnp.inf)
            best = jnp.max(blocks_of(raw), axis=1) + listed
            return jnp.maximum(top, jnp.max(best, axis=0, keepdims=True))

        return each(steps, one, jnp.full((1, QUERY_TILE), -jnp.inf, jnp.float32)) * factor

    def weigh(t, top):
        here = span(t, QUERY_TILE)
        held = score_ref.at[t % 2]

        def one(c, _):
            at = span(c, KEY_TILE)
            shift = bias_ref[c, :, here] - top
            e = jnp.exp2(blocks_of(held[at, :]) * factor + shift[:, None, :])
            w_ref[at, here] = e.reshape(KEY_TILE, QUERY_TILE).astype(w_ref.dtype)
            return 0

        each(steps, one, 0)

    def mix(t):
        here = span(t, QUERY_TILE)
        mixed = through(vt_ref, w_ref, here)
        inverse = 1.0 / mixed[HEAD_DIM : HEAD_DIM + 1]
        out = (mixed[:HEAD_DIM] * inverse).astype(jnp.bfloat16).astype(jnp.float32)
        put(out_at, t * QUERY_TILE, out.T)
        g = tile_of(g_at, t * QUERY_TILE, QUERY_TILE).astype(jnp.float32).T
        delta_ref[:, here] = jnp.sum(g * out, axis=0, keepdims=True) * inverse
        g = g * inverse
        gt_ref[:, here] = g.astype(gt_ref.dtype)
        gs_ref[here, :] = g.T.astype(gs_ref.dtype)

    tops = [score(0)]
    for t in range(turns):
        if t + 1 < turns:
            tops.append(score(t + 1))
        weigh(t, tops[t])
        mix(t)

    def backward(c, _):
        at = span(c, KEY_TILE)
        put(dv_at, c * KEY_TILE, dot(w_ref[at, :], gs_ref[...]))
        v = tile_of(v_at, c * KEY_TILE, KEY_TILE)
        for t in range(turns):
            here = span(t, QUERY_TILE)
            gap = dot(v, gt_ref[:, here]) - delta_ref[:, here]
            ds_ref[at, here] = (w_ref[at, here].astype(jnp.float32) * gap).astype(ds_ref.dtype)
        q = tile_of(q_at, 0, queries)
        put(dk_at, c * KEY_TILE, dot(ds_ref[at, :], q) * SCALE)
        return 0

    each(steps, backward, 0)
    flip(k_at, kt_ref, keys)
    for t in range(turns):
        put(dq_at, t * QUERY_TILE, (through(kt_ref, ds_ref, span(t, QUERY_TILE)) * SCALE).T)


def attend(rows, wide, random_blocks, global_blocks):
    team, _, height, _ = rows.shape
    queries = team * height
    apart = len(wide) > 0
    keys = wide[0].shape[0] * height if apart else queries
    outs = [jax.ShapeDtypeStruct((team, 2 if apart else 4, height, HEAD_DIM), rows.dtype)]
    if apart:
        outs += [jax.ShapeDtypeStruct(x.shape, jnp.float32) for x in wide]

    def kernel(*refs):
        rows_ref, *refs = refs
        k_at, v_at, dk_at, dv_at = (rows_ref, 2), (rows_ref, 3), None, None
        if apart:
            k_at, v_at, *refs = [(refs[0], 0), (refs[1], 0)] + refs[2:]
        random_ref, global_ref, out_ref, *refs = refs
        dk_at, dv_at = (out_ref, 2), (out_ref, 3)
        if apart:
            dk_at, dv_at, *refs = [(refs[0], 0), (refs[1], 0)] + refs[2:]
        score_ref, w_ref, *refs = refs
        ds_ref, *refs = [w_ref] + refs if apart else refs
        attend_kernel(
            (rows_ref, 0), (rows_ref, 1), k_at, v_at, random_ref, global_ref, (out_ref, 0), (out_ref, 1),
            dk_at, dv_at, score_ref, w_ref, ds_ref, *refs,
        )

    narrow = functools.partial(pltpu.VMEM, dtype=rows.dtype)
    ins = [rows, *wide, random_blocks, global_blocks]
    return pl.pallas_call(
        kernel,
        out_shape=outs,
        in_specs=[WHOLE] * len(ins),
        out_specs=[WHOLE] * len(outs),
        scratch_shapes=[pltpu.VMEM((2, keys, QUERY_TILE), jnp.float32)]
        + [narrow((keys, queries))] * (1 if apart else 2)
        + [
            pltpu.VMEM((keys // KEY_TILE, KEY_TILE // BLOCK, queries), jnp.float32),
            narrow((HEAD_DIM, keys)),
            narrow((HEAD_DIM + 16, keys)),
            narrow((HEAD_DIM, queries)),
            narrow((queries, HEAD_DIM)),
            pltpu.VMEM((1, queries), jnp.float32),
        ],
        compiler_params=pltpu.CompilerParams(vmem_limit_bytes=(60 if apart else 24) << 20),
    )(*ins)


def body(crews, team, queries, keys, values, grad_out, random_blocks, global_blocks):
    trade = functools.partial(
        lax.all_to_all, axis_name="lane", split_axis=0, concat_axis=0, tiled=True
    )
    tables = [random_blocks.transpose(2, 1, 0), global_blocks[None, :]]
    sent, *tables = pack([queries, grad_out, keys, values], tables)
    got = trade(sent)
    wide = []
    if crews > 1:
        wide = [lax.all_gather(got[:, a : a + 1], "crew", axis=0, tiled=True) for a in (2, 3)]
    back, *sums = attend(got, wide, *tables)
    sums = [lax.psum_scatter(x, "crew", scatter_dimension=0, tiled=True) for x in sums]
    if crews > 1:
        back = jnp.concatenate([back] + [x.astype(back.dtype) for x in sums], axis=1)
    return tuple(unpack(trade(back)))


def solution(mesh):
    devices = mesh.devices.reshape(-1)

    def run(queries, keys, values, grad_out, random_blocks, global_blocks):
        team = queries.shape[1] // HEAD_DIM
        crews = devices.size // team
        grid = Mesh(devices.reshape(crews, team), ("crew", "lane"))
        split = P(("crew", "lane"), None)
        return jax.shard_map(
            functools.partial(body, crews, team),
            mesh=grid,
            in_specs=(split,) * 4 + (P(), P()),
            out_specs=(split,) * 4,
            check_vma=False,
        )(queries, keys, values, grad_out, random_blocks, global_blocks)

    return run
```

time: 360 us -> 70.1 us (0.19)
  waiting for transfers between devices: 160 us -> 0 us
  starting transfers between devices: 80.1 us -> 0 us
  blocking collectives: 0 us -> 61.9 us
  local copies, waits for them, and re-layouts: 54.9 us -> 0 us
  matrix products: 24.8 us -> 0 us
  between operations: 20.1 us -> 0.65 us
  other arithmetic: 16.7 us -> 0 us
  Pallas kernels: 0 us -> 6.27 us
    psum x2 -> x0, waiting for transfers between devices: 110 us -> none  [the longest x1 56.2 us: spread_2(): return lax.psum(jnp.where(mine, shard, jnp.zeros_like(shard)), axis)]
    all_to_all x12 -> x0, starting transfers between devices: 68 us -> none  [the longest x1 17.1 us: body(): lax.all_to_all(keys_box, 'seq', split_axis=0, concat_axis=0, tiled=True)]
    all_to_all x0 -> x2, blocking collectives: none -> 61.9 us  [the longest x1 32.2 us: body(): got = trade(sent)]
    all_to_all x12 -> x0, waiting for transfers between devices: 36.6 us -> none  [the longest x1 11.1 us: body(): lax.all_to_all(value_send, 'seq', split_axis=0, concat_axis=0, tiled=True)]
    dot_general x20 -> x0, matrix products: 24.8 us -> none  [product(): jnp.einsum(formula, former, latter, preferred_element_type=jnp.float32)]
    scatter x2 -> x0, local copies, waits for them, and re-layouts: 14.4 us -> none  [the longest x1 7.63 us: body(): keys_box = tile_zero.at[my_owner, my_slot].set(rand_grad_keys)]
    ppermute x4 -> x0, waiting for transfers between devices: 13.9 us -> none  [the longest x2 7.58 us: extended(): after = lax.ppermute(first, axis, down)]
    ppermute x4 -> x0, starting transfers between devices: 12.1 us -> none  [the longest x2 9.41 us: extended(): before = lax.ppermute(last, axis, up)]
  transfers between devices with their start and end apart: 18 -> 0, of which waited for: 12 -> 0; matrix products, arithmetic and copies ran while one was open for 18% -> 0% of each run, Pallas kernels for 0% -> 0%
where the time goes in v1:
time: 70.1 us; the launch traced here: 68.8 us
  blocking collectives  61.9 us (88%)
  Pallas kernels  6.27 us (9%)
    all_to_all x1, blocking collectives, body(): got = trade(sent)  32.2 us
    all_to_all x1, blocking collectives, body(): return tuple(unpack(trade(back)))  29.7 us
    pallas_call x1, Pallas kernels, attend(): pl.pallas_call(kernel, out_shape=outs, in_specs=[WHOLE] * len(ins), out_s...  3.8 us
    pallas_call x1, Pallas kernels, pack(): pl.pallas_call(pack_kernel, out_shape=[pltpu.VMEM(shape, kind)] + [pltpu....  1.43 us

profile of v1, /device:TPU:1, one launch (start us, length us, event | category | flops | bytes accessed | tf_op | source)
XLA Modules:
  0.0 68.8 jit_solution(18313874015285772189)
XLA Ops:
  0.6 1.4 %shard_map.93 = (bf16[32,4,32,128]{3,2,1,0:T(8,128)(2,1)S(1)}, s32[3,16,32]{2,1,0:T(8,128)S(1)}, s32[1,2]{1,0:T(1,128)S(1)}) custom-call(s32[3,16,32]{2,1,0:T(8,128)} %bitcast.2, s32[1,2]{1,0:T(1,128)} %bitcast.3, bf16[32,4096]{1,0:T(8,128)(2,1)} %refs_0_.1, bf16[32,4096]{1,0:T(8,128)(2,1)} %refs_1_.1, bf16[32,4096]{1,0:T(8,128)(2,1)} %refs_2_.1, ...), custom_call_target="tpu_custom_call" | custom-call | tf_op jit(solution)/shard_map/pallas_call | solution.py:66
  2.1 32.2 %all_to_all.10.refs_0_ = bf16[32,4,32,128]{3,2,1,0:T(8,128)(2,1)S(1)} all-to-all(bf16[32,4,32,128]{3,2,1,0:T(8,128)(2,1)S(1)} %get-tuple-element.7), channel_id=1, replica_groups=mesh['seq'=8,'head'=4] {'seq','head'}, dimensions={0} | all-to-all | bytes 2097152 | tf_op jit(solution)/shard_map/all_to_all | solution.py:298
  34.3 3.8 %shard_map.94 = bf16[32,4,32,128]{3,2,1,0:T(8,128)(2,1)S(1)} custom-call(bf16[32,4,32,128]{3,2,1,0:T(8,128)(2,1)S(1)} %all_to_all.10.refs_0_, s32[3,16,32]{2,1,0:T(8,128)S(1)} %get-tuple-element.8.refs_1_, s32[1,2]{1,0:T(1,128)S(1)} %get-tuple-element.9.refs_2_), custom_call_target="tpu_custom_call" | custom-call | tf_op jit(solution)/shard_map/pallas_call | solution.py:273
  38.1 29.7 %all_to_all.11.packed = bf16[32,4,32,128]{3,2,1,0:T(8,128)(2,1)S(1)} all-to-all(bf16[32,4,32,128]{3,2,1,0:T(8,128)(2,1)S(1)} %shard_map.94), channel_id=1, replica_groups=mesh['seq'=8,'head'=4] {'seq','head'}, dimensions={0} | all-to-all | bytes 2097152 | tf_op jit(solution)/shard_map/all_to_all | solution.py:306
  67.8 1.0 %shard_map.95 = (bf16[32,4096]{1,0:T(8,128)(2,1)}, bf16[32,4096]{1,0:T(8,128)(2,1)}, bf16[32,4096]{1,0:T(8,128)(2,1)}, bf16[32,4096]{1,0:T(8,128)(2,1)}) custom-call(bf16[32,4,32,128]{3,2,1,0:T(8,128)(2,1)S(1)} %all_to_all.11.packed), custom_call_target="tpu_custom_call" | custom-call | tf_op jit(solution)/shard_map/pallas_call | solution.py:92

commit v2 on v1

--- a/solution.py
+++ b/solution.py
@@ -14,6 +14,7 @@
 SCALE = HEAD_DIM**-0.5
 QUERY_TILE = 256
 KEY_TILE = 512
+FAR_LANES = 4
 
 WHOLE = pl.BlockSpec(memory_space=pltpu.VMEM)
 FAR = pl.BlockSpec(memory_space=pltpu.HBM)
@@ -52,10 +53,12 @@
     *ins, out, random_out, global_out, held, sems = refs
     pairs = [(x, held.at[a]) for a, x in enumerate(ins)]
     pairs += [(random_ref, random_out), (global_ref, global_out)]
-    wait_all(copies(pairs, sems))
-    for h in range(out.shape[0]):
-        for a in range(len(ins)):
+    arriving = copies(pairs, sems)
+    for a in range(len(ins)):
+        arriving[a].wait()
+        for h in range(out.shape[0]):
             out[h, a] = held[a, :, h * HEAD_DIM : (h + 1) * HEAD_DIM]
+    wait_all(arriving[len(ins) :])
 
 
 def pack(arrays, tables):
@@ -102,29 +105,39 @@
     )(packed)
 
 
-def tile_of(pair, start, size):
-    ref, slot = pair
+def place(order, lane):
+    far, near = order
+    team = far * near
+    inside = lane % team
+    return lane - inside + inside % near * far + inside // near
+
+
+def tile_of(at, start, size):
+    ref, slot, order = at
     rows = ref.shape[2]
-    lanes = pl.ds(start // rows, size // rows)
-    return ref[lanes, slot].reshape(size, HEAD_DIM)
-
-
-def put(pair, start, tile):
-    ref, slot = pair
-    size, rows = tile.shape[0], ref.shape[2]
-    lanes = pl.ds(start // rows, size // rows)
-    ref[lanes, slot] = tile.astype(ref.dtype).reshape(size // rows, rows, HEAD_DIM)
+    first = start // rows
+    pieces = [ref[place(order, first + i), slot] for i in range(size // rows)]
+    return jnp.concatenate(pieces, axis=0)
+
+
+def put(at, start, tile):
+    ref, slot, order = at
+    rows = ref.shape[2]
+    first = start // rows
+    tile = tile.astype(ref.dtype)
+    for i in range(tile.shape[0] // rows):
+        ref[place(order, first + i), slot] = tile[i * rows : (i + 1) * rows]
 
 
 def span(i, size):
     return pl.ds(pl.multiple_of(i * size, size), size)
 
 
-def flip(pair, out, length):
+def flip(at, out, length):
     step = min(512, length)
 
     def one(i, _):
-        tile = tile_of(pair, i * step, step)
+        tile = tile_of(at, i * step, step)
         out[:HEAD_DIM, span(i, step)] = tile.astype(jnp.float32).T.astype(out.dtype)
         return 0
 
@@ -142,7 +155,8 @@
     for i in range(global_ref.shape[1]):
         times += (names == global_ref[:, i : i + 1]).astype(jnp.float32)
     heads = random_ref.shape[2]
-    mine = lax.broadcasted_iota(jnp.int32, (blocks, heads), 1) == lax.axis_index("lane")
+    head = lax.axis_index("near") * lax.axis_size("far") + lax.axis_index("far")
+    mine = lax.broadcasted_iota(jnp.int32, (blocks, heads), 1) == head
     for i in range(random_ref.shape[0]):
         picks = jnp.where(mine, random_ref[i, pl.ds(first, blocks), :], 0)
         times += (names == jnp.sum(picks, axis=1, keepdims=True)).astype(jnp.float32)
@@ -157,7 +171,7 @@
 
 def attend_kernel(
     q_at, g_at, k_at, v_at, random_ref, global_ref, out_at, dq_at, dk_at, dv_at,
-    score_ref, w_ref, ds_ref, bias_ref, kt_ref, vt_ref, gt_ref, gs_ref, delta_ref,
+    score_ref, w_ref, ds_ref, bias_ref, kt_ref, vt_ref, gt_ref, gs_ref, delta_ref, sum_ref,
 ):
     keys, queries = w_ref.shape
     steps = keys // KEY_TILE
@@ -181,7 +195,7 @@
 
     def score(t):
         here = span(t, QUERY_TILE)
-        held = score_ref.at[t % 2]
+        held = score_ref.at[t % score_ref.shape[0]]
         q = tile_of(q_at, t * QUERY_TILE, QUERY_TILE)
 
         def one(c, top):
@@ -195,7 +209,7 @@
 
     def weigh(t, top):
         here = span(t, QUERY_TILE)
-        held = score_ref.at[t % 2]
+        held = score_ref.at[t % score_ref.shape[0]]
 
         def one(c, _):
             at = span(c, KEY_TILE)
@@ -218,32 +232,69 @@
         gt_ref[:, here] = g.astype(gt_ref.dtype)
         gs_ref[here, :] = g.T.astype(gs_ref.dtype)
 
+    def back(t):
+        here = span(t, QUERY_TILE)
+
+        def one(c, _):
+            at = span(c, KEY_TILE)
+            gap = dot(tile_of(v_at, c * KEY_TILE, KEY_TILE), gt_ref[:, here]) - delta_ref[:, here]
+            ds_ref[at, here] = (w_ref[at, here].astype(jnp.float32) * gap).astype(ds_ref.dtype)
+            return 0
+
+        each(steps, one, 0)
+        put(dq_at, t * QUERY_TILE, (through(kt_ref, ds_ref, here) * SCALE).T)
+
+    def collect(left_ref, right, out_at, slot, scale, first, last):
+        here = pl.ds(first * QUERY_TILE, (last - first) * QUERY_TILE)
+
+        def one(c, _):
+            at = span(c, KEY_TILE)
+            total = dot(left_ref[at, here], right)
+            if first > 0:
+                total += sum_ref[slot, at, :] if sum_ref is not None else tile_of(out_at, c * KEY_TILE, KEY_TILE)
+            if last < turns and sum_ref is not None:
+                sum_ref[slot, at, :] = total
+            else:
+                put(out_at, c * KEY_TILE, total * scale if last == turns else total)
+            return 0
+
+        each(steps, one, 0)
+
+    def collect_values(first, last):
+        here = pl.ds(first * QUERY_TILE, (last - first) * QUERY_TILE)
+        collect(w_ref, gs_ref[here, :], dv_at, 0, 1.0, first, last)
+
+    def collect_keys(first, last):
+        q = tile_of(q_at, first * QUERY_TILE, (last - first) * QUERY_TILE)
+        collect(ds_ref, q, dk_at, 1, SCALE, first, last)
+
+    flip(k_at, kt_ref, keys)
+    if sum_ref is None:
+        for t in range(turns):
+            weigh(t, score(t))
+            mix(t)
+            collect_values(t, t + 1)
+            back(t)
+        collect_keys(0, turns)
+        return
+    half = turns // 2
     tops = [score(0)]
-    for t in range(turns):
+    for t in range(turns + 1):
         if t + 1 < turns:
             tops.append(score(t + 1))
-        weigh(t, tops[t])
-        mix(t)
-
-    def backward(c, _):
-        at = span(c, KEY_TILE)
-        put(dv_at, c * KEY_TILE, dot(w_ref[at, :], gs_ref[...]))
-        v = tile_of(v_at, c * KEY_TILE, KEY_TILE)
-        for t in range(turns):
-            here = span(t, QUERY_TILE)
-            gap = dot(v, gt_ref[:, here]) - delta_ref[:, here]
-            ds_ref[at, here] = (w_ref[at, here].astype(jnp.float32) * gap).astype(ds_ref.dtype)
-        q = tile_of(q_at, 0, queries)
-        put(dk_at, c * KEY_TILE, dot(ds_ref[at, :], q) * SCALE)
-        return 0
-
-    each(steps, backward, 0)
-    flip(k_at, kt_ref, keys)
-    for t in range(turns):
-        put(dq_at, t * QUERY_TILE, (through(kt_ref, ds_ref, span(t, QUERY_TILE)) * SCALE).T)
-
-
-def attend(rows, wide, random_blocks, global_blocks):
+        if t < turns:
+            weigh(t, tops[t])
+            mix(t)
+        if t > 0:
+            back(t - 1)
+        if t == half:
+            collect_values(0, half)
+            collect_keys(0, half)
+    collect_values(half, turns)
+    collect_keys(half, turns)
+
+
+def attend(rows, wide, random_blocks, global_blocks, order):
     team, _, height, _ = rows.shape
     queries = team * height
     apart = len(wide) > 0
@@ -254,18 +305,18 @@
 
     def kernel(*refs):
         rows_ref, *refs = refs
-        k_at, v_at, dk_at, dv_at = (rows_ref, 2), (rows_ref, 3), None, None
+        q_at, g_at, k_at, v_at = ((rows_ref, a, order) for a in range(4))
         if apart:
-            k_at, v_at, *refs = [(refs[0], 0), (refs[1], 0)] + refs[2:]
+            k_at, v_at, *refs = [(refs[0], 0, order), (refs[1], 0, order)] + refs[2:]
         random_ref, global_ref, out_ref, *refs = refs
-        dk_at, dv_at = (out_ref, 2), (out_ref, 3)
+        out_at, dq_at, dk_at, dv_at = ((out_ref, a, order) for a in range(4))
         if apart:
-            dk_at, dv_at, *refs = [(refs[0], 0), (refs[1], 0)] + refs[2:]
+            dk_at, dv_at, *refs = [(refs[0], 0, order), (refs[1], 0, order)] + refs[2:]
         score_ref, w_ref, *refs = refs
         ds_ref, *refs = [w_ref] + refs if apart else refs
         attend_kernel(
-            (rows_ref, 0), (rows_ref, 1), k_at, v_at, random_ref, global_ref, (out_ref, 0), (out_ref, 1),
-            dk_at, dv_at, score_ref, w_ref, ds_ref, *refs,
+            q_at, g_at, k_at, v_at, random_ref, global_ref, out_at, dq_at, dk_at, dv_at,
+            score_ref, w_ref, ds_ref, *refs[:6], *(refs[6:] or [None]),
         )
 
     narrow = functools.partial(pltpu.VMEM, dtype=rows.dtype)
@@ -275,7 +326,7 @@
         out_shape=outs,
         in_specs=[WHOLE] * len(ins),
         out_specs=[WHOLE] * len(outs),
-        scratch_shapes=[pltpu.VMEM((2, keys, QUERY_TILE), jnp.float32)]
+        scratch_shapes=[pltpu.VMEM((1 if apart else 2, keys, QUERY_TILE), jnp.float32)]
         + [narrow((keys, queries))] * (1 if apart else 2)
         + [
             pltpu.VMEM((keys // KEY_TILE, KEY_TILE // BLOCK, queries), jnp.float32),
@@ -284,14 +335,15 @@
             narrow((HEAD_DIM, queries)),
             narrow((queries, HEAD_DIM)),
             pltpu.VMEM((1, queries), jnp.float32),
-        ],
+        ]
+        + [pltpu.VMEM((2, keys, HEAD_DIM), jnp.float32)] * (not apart),
         compiler_params=pltpu.CompilerParams(vmem_limit_bytes=(60 if apart else 24) << 20),
     )(*ins)
 
 
-def body(crews, team, queries, keys, values, grad_out, random_blocks, global_blocks):
+def body(crews, order, queries, keys, values, grad_out, random_blocks, global_blocks):
     trade = functools.partial(
-        lax.all_to_all, axis_name="lane", split_axis=0, concat_axis=0, tiled=True
+        lax.all_to_all, axis_name=("near", "far"), split_axis=0, concat_axis=0, tiled=True
     )
     tables = [random_blocks.transpose(2, 1, 0), global_blocks[None, :]]
     sent, *tables = pack([queries, grad_out, keys, values], tables)
@@ -299,7 +351,7 @@
     wide = []
     if crews > 1:
         wide = [lax.all_gather(got[:, a : a + 1], "crew", axis=0, tiled=True) for a in (2, 3)]
-    back, *sums = attend(got, wide, *tables)
+    back, *sums = attend(got, wide, *tables, order)
     sums = [lax.psum_scatter(x, "crew", scatter_dimension=0, tiled=True) for x in sums]
     if crews > 1:
         back = jnp.concatenate([back] + [x.astype(back.dtype) for x in sums], axis=1)
@@ -312,10 +364,11 @@
     def run(queries, keys, values, grad_out, random_blocks, global_blocks):
         team = queries.shape[1] // HEAD_DIM
         crews = devices.size // team
-        grid = Mesh(devices.reshape(crews, team), ("crew", "lane"))
-        split = P(("crew", "lane"), None)
+        order = (FAR_LANES, team // FAR_LANES)
+        grid = Mesh(devices.reshape(crews, *order), ("crew", "far", "near"))
+        split = P(("crew", "far", "near"), None)
         return jax.shard_map(
-            functools.partial(body, crews, team),
+            functools.partial(body, crews, order),
             mesh=grid,
             in_specs=(split,) * 4 + (P(), P()),
             out_specs=(split,) * 4,

time: 70.1 us -> 69.9 us (level); the launches traced: 68.8 us -> 69.7 us
    all_to_all x1, blocking collectives: 32.2 us -> 33.3 us  [body(): got = trade(sent)]
where the time goes in v2:
time: 69.9 us; the launch traced here: 69.7 us
  blocking collectives  62.6 us (90%)
  Pallas kernels  6.48 us (9%)
    all_to_all x1, blocking collectives, body(): got = trade(sent)  33.3 us
    all_to_all x1, blocking collectives, body(): return tuple(unpack(trade(back)))  29.3 us
    pallas_call x1, Pallas kernels, attend(): pl.pallas_call(kernel, out_shape=outs, in_specs=[WHOLE] * len(ins), out_s...  4.15 us

profile of v2, /device:TPU:1, one launch (start us, length us, event | category | flops | bytes accessed | tf_op | source)
XLA Modules:
  0.0 69.7 jit_solution(13524660295121251252)
XLA Ops:
  0.6 1.3 %shard_map.93 = (bf16[32,4,32,128]{3,2,1,0:T(8,128)(2,1)S(1)}, s32[3,16,32]{2,1,0:T(8,128)S(1)}, s32[1,2]{1,0:T(1,128)S(1)}) custom-call(s32[3,16,32]{2,1,0:T(8,128)} %bitcast.2, s32[1,2]{1,0:T(1,128)} %bitcast.3, bf16[32,4096]{1,0:T(8,128)(2,1)} %refs_0_.1, bf16[32,4096]{1,0:T(8,128)(2,1)} %refs_1_.1, bf16[32,4096]{1,0:T(8,128)(2,1)} %refs_2_.1, ...), custom_call_target="tpu_custom_call" | custom-call | tf_op jit(solution)/shard_map/pallas_call | solution.py:69
  1.9 33.3 %all_to_all.10.refs_0_ = bf16[32,4,32,128]{3,2,1,0:T(8,128)(2,1)S(1)} all-to-all(bf16[32,4,32,128]{3,2,1,0:T(8,128)(2,1)S(1)} %get-tuple-element.7), channel_id=1, replica_groups=mesh['seq'=8,'head'=4] {'seq':(4)2,'head','seq':(1)4}, dimensions={0} | all-to-all | bytes 2097152 | tf_op jit(solution)/shard_map/all_to_all | solution.py:350
  35.2 4.1 %shard_map.94 = bf16[32,4,32,128]{3,2,1,0:T(8,128)(2,1)S(1)} custom-call(bf16[32,4,32,128]{3,2,1,0:T(8,128)(2,1)S(1)} %all_to_all.10.refs_0_, s32[3,16,32]{2,1,0:T(8,128)S(1)} %get-tuple-element.8.refs_1_, s32[1,2]{1,0:T(1,128)S(1)} %get-tuple-element.9.refs_2_), custom_call_target="tpu_custom_call" | custom-call | tf_op jit(solution)/shard_map/pallas_call | solution.py:324
  39.4 29.3 %all_to_all.11.packed = bf16[32,4,32,128]{3,2,1,0:T(8,128)(2,1)S(1)} all-to-all(bf16[32,4,32,128]{3,2,1,0:T(8,128)(2,1)S(1)} %shard_map.94), channel_id=1, replica_groups=mesh['seq'=8,'head'=4] {'seq':(4)2,'head','seq':(1)4}, dimensions={0} | all-to-all | bytes 2097152 | tf_op jit(solution)/shard_map/all_to_all | solution.py:358
  68.7 1.0 %shard_map.95 = (bf16[32,4096]{1,0:T(8,128)(2,1)}, bf16[32,4096]{1,0:T(8,128)(2,1)}, bf16[32,4096]{1,0:T(8,128)(2,1)}, bf16[32,4096]{1,0:T(8,128)(2,1)}) custom-call(bf16[32,4,32,128]{3,2,1,0:T(8,128)(2,1)S(1)} %all_to_all.11.packed), custom_call_target="tpu_custom_call" | custom-call | tf_op jit(solution)/shard_map/pallas_call | solution.py:95

commit v3 on v1

--- a/solution.py
+++ b/solution.py
@@ -14,6 +14,7 @@
 SCALE = HEAD_DIM**-0.5
 QUERY_TILE = 256
 KEY_TILE = 512
+FAR_LANES = 4
 
 WHOLE = pl.BlockSpec(memory_space=pltpu.VMEM)
 FAR = pl.BlockSpec(memory_space=pltpu.HBM)
@@ -52,10 +53,12 @@
     *ins, out, random_out, global_out, held, sems = refs
     pairs = [(x, held.at[a]) for a, x in enumerate(ins)]
     pairs += [(random_ref, random_out), (global_ref, global_out)]
-    wait_all(copies(pairs, sems))
-    for h in range(out.shape[0]):
-        for a in range(len(ins)):
+    arriving = copies(pairs, sems)
+    for a in range(len(ins)):
+        arriving[a].wait()
+        for h in range(out.shape[0]):
             out[h, a] = held[a, :, h * HEAD_DIM : (h + 1) * HEAD_DIM]
+    wait_all(arriving[len(ins) :])
 
 
 def pack(arrays, tables):
@@ -102,30 +105,46 @@
     )(packed)
 
 
-def tile_of(pair, start, size):
-    ref, slot = pair
+def place(order, lane):
+    far, near = order
+    team = far * near
+    inside = lane % team
+    return lane - inside + inside % near * far + inside // near
+
+
+def tile_of(at, start, size):
+    ref, slot, order = at
     rows = ref.shape[2]
-    lanes = pl.ds(start // rows, size // rows)
-    return ref[lanes, slot].reshape(size, HEAD_DIM)
-
-
-def put(pair, start, tile):
-    ref, slot = pair
-    size, rows = tile.shape[0], ref.shape[2]
-    lanes = pl.ds(start // rows, size // rows)
-    ref[lanes, slot] = tile.astype(ref.dtype).reshape(size // rows, rows, HEAD_DIM)
+    first = start // rows
+    pieces = [ref[place(order, first + i), slot] for i in range(size // rows)]
+    return jnp.concatenate(pieces, axis=0)
+
+
+def put(at, start, tile):
+    ref, slot, order = at
+    rows = ref.shape[2]
+    first = start // rows
+    tile = tile.astype(ref.dtype)
+    for i in range(tile.shape[0] // rows):
+        ref[place(order, first + i), slot] = tile[i * rows : (i + 1) * rows]
 
 
 def span(i, size):
     return pl.ds(pl.multiple_of(i * size, size), size)
 
 
-def flip(pair, out, length):
+def turned(x):
+    size = (x.shape[1], x.shape[1])
+    same = lax.broadcasted_iota(jnp.int32, size, 0) == lax.broadcasted_iota(jnp.int32, size, 1)
+    return dot_nt(same.astype(x.dtype), x)
+
+
+def flip(at, out, length):
     step = min(512, length)
 
     def one(i, _):
-        tile = tile_of(pair, i * step, step)
-        out[:HEAD_DIM, span(i, step)] = tile.astype(jnp.float32).T.astype(out.dtype)
+        tile = tile_of(at, i * step, step)
+        out[:HEAD_DIM, span(i, step)] = turned(tile).astype(out.dtype)
         return 0
 
     each(length // step, one, 0)
@@ -142,7 +161,8 @@
     for i in range(global_ref.shape[1]):
         times += (names == global_ref[:, i : i + 1]).astype(jnp.float32)
     heads = random_ref.shape[2]
-    mine = lax.broadcasted_iota(jnp.int32, (blocks, heads), 1) == lax.axis_index("lane")
+    head = lax.axis_index("near") * lax.axis_size("far") + lax.axis_index("far")
+    mine = lax.broadcasted_iota(jnp.int32, (blocks, heads), 1) == head
     for i in range(random_ref.shape[0]):
         picks = jnp.where(mine, random_ref[i, pl.ds(first, blocks), :], 0)
         times += (names == jnp.sum(picks, axis=1, keepdims=True)).astype(jnp.float32)
@@ -210,13 +230,14 @@
         here = span(t, QUERY_TILE)
         mixed = through(vt_ref, w_ref, here)
         inverse = 1.0 / mixed[HEAD_DIM : HEAD_DIM + 1]
-        out = (mixed[:HEAD_DIM] * inverse).astype(jnp.bfloat16).astype(jnp.float32)
-        put(out_at, t * QUERY_TILE, out.T)
-        g = tile_of(g_at, t * QUERY_TILE, QUERY_TILE).astype(jnp.float32).T
+        out = (mixed[:HEAD_DIM] * inverse).astype(jnp.bfloat16)
+        put(out_at, t * QUERY_TILE, turned(out))
+        out = out.astype(jnp.float32)
+        g = turned(tile_of(g_at, t * QUERY_TILE, QUERY_TILE))
         delta_ref[:, here] = jnp.sum(g * out, axis=0, keepdims=True) * inverse
-        g = g * inverse
-        gt_ref[:, here] = g.astype(gt_ref.dtype)
-        gs_ref[here, :] = g.T.astype(gs_ref.dtype)
+        g = (g * inverse).astype(gt_ref.dtype)
+        gt_ref[:, here] = g
+        gs_ref[here, :] = turned(g).astype(gs_ref.dtype)
 
     tops = [score(0)]
     for t in range(turns):
@@ -240,10 +261,11 @@
     each(steps, backward, 0)
     flip(k_at, kt_ref, keys)
     for t in range(turns):
-        put(dq_at, t * QUERY_TILE, (through(kt_ref, ds_ref, span(t, QUERY_TILE)) * SCALE).T)
-
-
-def attend(rows, wide, random_blocks, global_blocks):
+        dq = through(kt_ref, ds_ref, span(t, QUERY_TILE)) * SCALE
+        put(dq_at, t * QUERY_TILE, turned(dq.astype(jnp.bfloat16)))
+
+
+def attend(rows, wide, random_blocks, global_blocks, order):
     team, _, height, _ = rows.shape
     queries = team * height
     apart = len(wide) > 0
@@ -254,18 +276,18 @@
 
     def kernel(*refs):
         rows_ref, *refs = refs
-        k_at, v_at, dk_at, dv_at = (rows_ref, 2), (rows_ref, 3), None, None
+        q_at, g_at, k_at, v_at = ((rows_ref, a, order) for a in range(4))
         if apart:
-            k_at, v_at, *refs = [(refs[0], 0), (refs[1], 0)] + refs[2:]
+            k_at, v_at, *refs = [(refs[0], 0, order), (refs[1], 0, order)] + refs[2:]
         random_ref, global_ref, out_ref, *refs = refs
-        dk_at, dv_at = (out_ref, 2), (out_ref, 3)
+        out_at, dq_at, dk_at, dv_at = ((out_ref, a, order) for a in range(4))
         if apart:
-            dk_at, dv_at, *refs = [(refs[0], 0), (refs[1], 0)] + refs[2:]
+            dk_at, dv_at, *refs = [(refs[0], 0, order), (refs[1], 0, order)] + refs[2:]
         score_ref, w_ref, *refs = refs
         ds_ref, *refs = [w_ref] + refs if apart else refs
         attend_kernel(
-            (rows_ref, 0), (rows_ref, 1), k_at, v_at, random_ref, global_ref, (out_ref, 0), (out_ref, 1),
-            dk_at, dv_at, score_ref, w_ref, ds_ref, *refs,
+            q_at, g_at, k_at, v_at, random_ref, global_ref, out_at, dq_at, dk_at, dv_at,
+            score_ref, w_ref, ds_ref, *refs,
         )
 
     narrow = functools.partial(pltpu.VMEM, dtype=rows.dtype)
@@ -289,9 +311,9 @@
     )(*ins)
 
 
-def body(crews, team, queries, keys, values, grad_out, random_blocks, global_blocks):
+def body(crews, order, queries, keys, values, grad_out, random_blocks, global_blocks):
     trade = functools.partial(
-        lax.all_to_all, axis_name="lane", split_axis=0, concat_axis=0, tiled=True
+        lax.all_to_all, axis_name=("near", "far"), split_axis=0, concat_axis=0, tiled=True
     )
     tables = [random_blocks.transpose(2, 1, 0), global_blocks[None, :]]
     sent, *tables = pack([queries, grad_out, keys, values], tables)
@@ -299,7 +321,7 @@
     wide = []
     if crews > 1:
         wide = [lax.all_gather(got[:, a : a + 1], "crew", axis=0, tiled=True) for a in (2, 3)]
-    back, *sums = attend(got, wide, *tables)
+    back, *sums = attend(got, wide, *tables, order)
     sums = [lax.psum_scatter(x, "crew", scatter_dimension=0, tiled=True) for x in sums]
     if crews > 1:
         back = jnp.concatenate([back] + [x.astype(back.dtype) for x in sums], axis=1)
@@ -312,10 +334,11 @@
     def run(queries, keys, values, grad_out, random_blocks, global_blocks):
         team = queries.shape[1] // HEAD_DIM
         crews = devices.size // team
-        grid = Mesh(devices.reshape(crews, team), ("crew", "lane"))
-        split = P(("crew", "lane"), None)
+        order = (FAR_LANES, team // FAR_LANES)
+        grid = Mesh(devices.reshape(crews, *order), ("crew", "far", "near"))
+        split = P(("crew", "far", "near"), None)
         return jax.shard_map(
-            functools.partial(body, crews, team),
+            functools.partial(body, crews, order),
             mesh=grid,
             in_specs=(split,) * 4 + (P(), P()),
             out_specs=(split,) * 4,

time: 70.1 us -> 71.2 us (1.016); the launches traced: 68.8 us -> 71.1 us
  Pallas kernels: 6.27 us -> 7.83 us
    pallas_call x1, Pallas kernels: 3.8 us -> 5.5 us  [attend(): pl.pallas_call(kernel, out_shape=outs, in_specs=[WHOLE] * len(ins), out_s...]
    all_to_all x1, blocking collectives: 32.2 us -> 33.3 us  [body(): got = trade(sent)]
where the time goes in v3:
time: 71.2 us; the launch traced here: 71.1 us
  blocking collectives  62.6 us (88%)
  Pallas kernels  7.83 us (11%)
    all_to_all x1, blocking collectives, body(): got = trade(sent)  33.3 us
    all_to_all x1, blocking collectives, body(): return tuple(unpack(trade(back)))  29.3 us
    pallas_call x1, Pallas kernels, attend(): pl.pallas_call(kernel, out_shape=outs, in_specs=[WHOLE] * len(ins), out_s...  5.5 us

profile of v3, /device:TPU:1, one launch (start us, length us, event | category | flops | bytes accessed | tf_op | source)
XLA Modules:
  0.0 71.1 jit_solution(10831897312874398082)
XLA Ops:
  0.6 1.3 %shard_map.93 = (bf16[32,4,32,128]{3,2,1,0:T(8,128)(2,1)S(1)}, s32[3,16,32]{2,1,0:T(8,128)S(1)}, s32[1,2]{1,0:T(1,128)S(1)}) custom-call(s32[3,16,32]{2,1,0:T(8,128)} %bitcast.2, s32[1,2]{1,0:T(1,128)} %bitcast.3, bf16[32,4096]{1,0:T(8,128)(2,1)} %refs_0_.1, bf16[32,4096]{1,0:T(8,128)(2,1)} %refs_1_.1, bf16[32,4096]{1,0:T(8,128)(2,1)} %refs_2_.1, ...), custom_call_target="tpu_custom_call" | custom-call | tf_op jit(solution)/shard_map/pallas_call | solution.py:69
  1.9 33.3 %all_to_all.10.refs_0_ = bf16[32,4,32,128]{3,2,1,0:T(8,128)(2,1)S(1)} all-to-all(bf16[32,4,32,128]{3,2,1,0:T(8,128)(2,1)S(1)} %get-tuple-element.7), channel_id=1, replica_groups=mesh['seq'=8,'head'=4] {'seq':(4)2,'head','seq':(1)4}, dimensions={0} | all-to-all | bytes 2097152 | tf_op jit(solution)/shard_map/all_to_all | solution.py:320
  35.2 5.5 %shard_map.94 = bf16[32,4,32,128]{3,2,1,0:T(8,128)(2,1)S(1)} custom-call(bf16[32,4,32,128]{3,2,1,0:T(8,128)(2,1)S(1)} %all_to_all.10.refs_0_, s32[3,16,32]{2,1,0:T(8,128)S(1)} %get-tuple-element.8.refs_1_, s32[1,2]{1,0:T(1,128)S(1)} %get-tuple-element.9.refs_2_), custom_call_target="tpu_custom_call" | custom-call | tf_op jit(solution)/shard_map/pallas_call | solution.py:295
  40.7 29.3 %all_to_all.11.packed = bf16[32,4,32,128]{3,2,1,0:T(8,128)(2,1)S(1)} all-to-all(bf16[32,4,32,128]{3,2,1,0:T(8,128)(2,1)S(1)} %shard_map.94), channel_id=1, replica_groups=mesh['seq'=8,'head'=4] {'seq':(4)2,'head','seq':(1)4}, dimensions={0} | all-to-all | bytes 2097152 | tf_op jit(solution)/shard_map/all_to_all | solution.py:328
  70.0 1.0 %shard_map.95 = (bf16[32,4096]{1,0:T(8,128)(2,1)}, bf16[32,4096]{1,0:T(8,128)(2,1)}, bf16[32,4096]{1,0:T(8,128)(2,1)}, bf16[32,4096]{1,0:T(8,128)(2,1)}) custom-call(bf16[32,4,32,128]{3,2,1,0:T(8,128)(2,1)S(1)} %all_to_all.11.packed), custom_call_target="tpu_custom_call" | custom-call | tf_op jit(solution)/shard_map/pallas_call | solution.py:95

commit v4 on v3

--- a/solution.py
+++ b/solution.py
@@ -22,10 +22,6 @@
 
 def dot(a, b):
     return lax.dot_general(a, b, (((1,), (0,)), ((), ())), preferred_element_type=jnp.float32)
-
-
-def dot_nt(a, b):
-    return lax.dot_general(a, b, (((1,), (1,)), ((), ())), preferred_element_type=jnp.float32)
 
 
 def each(count, step, start):
@@ -133,18 +129,12 @@
     return pl.ds(pl.multiple_of(i * size, size), size)
 
 
-def turned(x):
-    size = (x.shape[1], x.shape[1])
-    same = lax.broadcasted_iota(jnp.int32, size, 0) == lax.broadcasted_iota(jnp.int32, size, 1)
-    return dot_nt(same.astype(x.dtype), x)
-
-
 def flip(at, out, length):
     step = min(512, length)
 
     def one(i, _):
         tile = tile_of(at, i * step, step)
-        out[:HEAD_DIM, span(i, step)] = turned(tile).astype(out.dtype)
+        out[:HEAD_DIM, span(i, step)] = tile.astype(jnp.float32).T.astype(out.dtype)
         return 0
 
     each(length // step, one, 0)
@@ -202,10 +192,10 @@
     def score(t):
         here = span(t, QUERY_TILE)
         held = score_ref.at[t % 2]
-        q = tile_of(q_at, t * QUERY_TILE, QUERY_TILE)
+        q = tile_of(q_at, t * QUERY_TILE, QUERY_TILE).astype(jnp.float32).T.astype(jnp.bfloat16)
 
         def one(c, top):
-            raw = dot_nt(tile_of(k_at, c * KEY_TILE, KEY_TILE), q)
+            raw = dot(tile_of(k_at, c * KEY_TILE, KEY_TILE), q)
             held[span(c, KEY_TILE), :] = raw
             listed = jnp.where(bias_ref[c, :, here] > -jnp.inf, 0.0, -jnp.inf)
             best = jnp.max(blocks_of(raw), axis=1) + listed
@@ -230,14 +220,13 @@
         here = span(t, QUERY_TILE)
         mixed = through(vt_ref, w_ref, here)
         inverse = 1.0 / mixed[HEAD_DIM : HEAD_DIM + 1]
-        out = (mixed[:HEAD_DIM] * inverse).astype(jnp.bfloat16)
-        put(out_at, t * QUERY_TILE, turned(out))
-        out = out.astype(jnp.float32)
-        g = turned(tile_of(g_at, t * QUERY_TILE, QUERY_TILE))
+        out = (mixed[:HEAD_DIM] * inverse).astype(jnp.bfloat16).astype(jnp.float32)
+        put(out_at, t * QUERY_TILE, out.T)
+        g = tile_of(g_at, t * QUERY_TILE, QUERY_TILE).astype(jnp.float32).T
         delta_ref[:, here] = jnp.sum(g * out, axis=0, keepdims=True) * inverse
-        g = (g * inverse).astype(gt_ref.dtype)
-        gt_ref[:, here] = g
-        gs_ref[here, :] = turned(g).astype(gs_ref.dtype)
+        g = g * inverse
+        gt_ref[:, here] = g.astype(gt_ref.dtype)
+        gs_ref[here, :] = g.T.astype(gs_ref.dtype)
 
     tops = [score(0)]
     for t in range(turns):
@@ -261,8 +250,7 @@
     each(steps, backward, 0)
     flip(k_at, kt_ref, keys)
     for t in range(turns):
-        dq = through(kt_ref, ds_ref, span(t, QUERY_TILE)) * SCALE
-        put(dq_at, t * QUERY_TILE, turned(dq.astype(jnp.bfloat16)))
+        put(dq_at, t * QUERY_TILE, (through(kt_ref, ds_ref, span(t, QUERY_TILE)) * SCALE).T)
 
 
 def attend(rows, wide, random_blocks, global_blocks, order):

time: 71.2 us -> 69.6 us (0.978)
  Pallas kernels: 7.83 us -> 6.19 us
    pallas_call x1, Pallas kernels: 5.5 us -> 3.86 us  [attend(): pl.pallas_call(kernel, out_shape=outs, in_specs=[WHOLE] * len(ins), out_s...]
where the time goes in v4:
time: 69.6 us; the launch traced here: 69.4 us
  blocking collectives  62.6 us (90%)
  Pallas kernels  6.19 us (9%)
    all_to_all x1, blocking collectives, body(): got = trade(sent)  33.3 us
    all_to_all x1, blocking collectives, body(): return tuple(unpack(trade(back)))  29.3 us
    pallas_call x1, Pallas kernels, attend(): pl.pallas_call(kernel, out_shape=outs, in_specs=[WHOLE] * len(ins), out_s...  3.86 us

profile of v4, /device:TPU:1, one launch (start us, length us, event | category | flops | bytes accessed | tf_op | source)
XLA Modules:
  0.0 69.4 jit_solution(6570683662469514510)
XLA Ops:
  0.6 1.3 %shard_map.93 = (bf16[32,4,32,128]{3,2,1,0:T(8,128)(2,1)S(1)}, s32[3,16,32]{2,1,0:T(8,128)S(1)}, s32[1,2]{1,0:T(1,128)S(1)}) custom-call(s32[3,16,32]{2,1,0:T(8,128)} %bitcast.2, s32[1,2]{1,0:T(1,128)} %bitcast.3, bf16[32,4096]{1,0:T(8,128)(2,1)} %refs_0_.1, bf16[32,4096]{1,0:T(8,128)(2,1)} %refs_1_.1, bf16[32,4096]{1,0:T(8,128)(2,1)} %refs_2_.1, ...), custom_call_target="tpu_custom_call" | custom-call | tf_op jit(solution)/shard_map/pallas_call | solution.py:65
  1.9 33.3 %all_to_all.10.refs_0_ = bf16[32,4,32,128]{3,2,1,0:T(8,128)(2,1)S(1)} all-to-all(bf16[32,4,32,128]{3,2,1,0:T(8,128)(2,1)S(1)} %get-tuple-element.7), channel_id=1, replica_groups=mesh['seq'=8,'head'=4] {'seq':(4)2,'head','seq':(1)4}, dimensions={0} | all-to-all | bytes 2097152 | tf_op jit(solution)/shard_map/all_to_all | solution.py:308
  35.2 3.9 %shard_map.94 = bf16[32,4,32,128]{3,2,1,0:T(8,128)(2,1)S(1)} custom-call(bf16[32,4,32,128]{3,2,1,0:T(8,128)(2,1)S(1)} %all_to_all.10.refs_0_, s32[3,16,32]{2,1,0:T(8,128)S(1)} %get-tuple-element.8.refs_1_, s32[1,2]{1,0:T(1,128)S(1)} %get-tuple-element.9.refs_2_), custom_call_target="tpu_custom_call" | custom-call | tf_op jit(solution)/shard_map/pallas_call | solution.py:283
  39.1 29.3 %all_to_all.11.packed = bf16[32,4,32,128]{3,2,1,0:T(8,128)(2,1)S(1)} all-to-all(bf16[32,4,32,128]{3,2,1,0:T(8,128)(2,1)S(1)} %shard_map.94), channel_id=1, replica_groups=mesh['seq'=8,'head'=4] {'seq':(4)2,'head','seq':(1)4}, dimensions={0} | all-to-all | bytes 2097152 | tf_op jit(solution)/shard_map/all_to_all | solution.py:316
  68.4 1.0 %shard_map.95 = (bf16[32,4096]{1,0:T(8,128)(2,1)}, bf16[32,4096]{1,0:T(8,128)(2,1)}, bf16[32,4096]{1,0:T(8,128)(2,1)}, bf16[32,4096]{1,0:T(8,128)(2,1)}) custom-call(bf16[32,4,32,128]{3,2,1,0:T(8,128)(2,1)S(1)} %all_to_all.11.packed), custom_call_target="tpu_custom_call" | custom-call | tf_op jit(solution)/shard_map/pallas_call | solution.py:91

commit v5 on v4

--- a/solution.py
+++ b/solution.py
@@ -13,7 +13,7 @@
 BLOCK = 64
 SCALE = HEAD_DIM**-0.5
 QUERY_TILE = 256
-KEY_TILE = 512
+KEY_TILE = 1024
 FAR_LANES = 4
 
 WHOLE = pl.BlockSpec(memory_space=pltpu.VMEM)

time: 69.6 us -> 69.6 us (level)
  no operation moved by 1% of the time
where the time goes in v5:
time: 69.6 us; the launch traced here: 69.4 us
  blocking collectives  62.6 us (90%)
  Pallas kernels  6.15 us (9%)
    all_to_all x1, blocking collectives, body(): got = trade(sent)  33.3 us
    all_to_all x1, blocking collectives, body(): return tuple(unpack(trade(back)))  29.3 us
    pallas_call x1, Pallas kernels, attend(): pl.pallas_call(kernel, out_shape=outs, in_specs=[WHOLE] * len(ins), out_s...  3.82 us

profile of v5, /device:TPU:1, one launch (start us, length us, event | category | flops | bytes accessed | tf_op | source)
XLA Modules:
  0.0 69.4 jit_solution(8837767019390179002)
XLA Ops:
  0.6 1.3 %shard_map.93 = (bf16[32,4,32,128]{3,2,1,0:T(8,128)(2,1)S(1)}, s32[3,16,32]{2,1,0:T(8,128)S(1)}, s32[1,2]{1,0:T(1,128)S(1)}) custom-call(s32[3,16,32]{2,1,0:T(8,128)} %bitcast.2, s32[1,2]{1,0:T(1,128)} %bitcast.3, bf16[32,4096]{1,0:T(8,128)(2,1)} %refs_0_.1, bf16[32,4096]{1,0:T(8,128)(2,1)} %refs_1_.1, bf16[32,4096]{1,0:T(8,128)(2,1)} %refs_2_.1, ...), custom_call_target="tpu_custom_call" | custom-call | tf_op jit(solution)/shard_map/pallas_call | solution.py:65
  1.9 33.3 %all_to_all.10.refs_0_ = bf16[32,4,32,128]{3,2,1,0:T(8,128)(2,1)S(1)} all-to-all(bf16[32,4,32,128]{3,2,1,0:T(8,128)(2,1)S(1)} %get-tuple-element.7), channel_id=1, replica_groups=mesh['seq'=8,'head'=4] {'seq':(4)2,'head','seq':(1)4}, dimensions={0} | all-to-all | bytes 2097152 | tf_op jit(solution)/shard_map/all_to_all | solution.py:308
  35.2 3.8 %shard_map.94 = bf16[32,4,32,128]{3,2,1,0:T(8,128)(2,1)S(1)} custom-call(bf16[32,4,32,128]{3,2,1,0:T(8,128)(2,1)S(1)} %all_to_all.10.refs_0_, s32[3,16,32]{2,1,0:T(8,128)S(1)} %get-tuple-element.8.refs_1_, s32[1,2]{1,0:T(1,128)S(1)} %get-tuple-element.9.refs_2_), custom_call_target="tpu_custom_call" | custom-call | tf_op jit(solution)/shard_map/pallas_call | solution.py:283
  39.0 29.3 %all_to_all.11.packed = bf16[32,4,32,128]{3,2,1,0:T(8,128)(2,1)S(1)} all-to-all(bf16[32,4,32,128]{3,2,1,0:T(8,128)(2,1)S(1)} %shard_map.94), channel_id=1, replica_groups=mesh['seq'=8,'head'=4] {'seq':(4)2,'head','seq':(1)4}, dimensions={0} | all-to-all | bytes 2097152 | tf_op jit(solution)/shard_map/all_to_all | solution.py:316
  68.3 1.0 %shard_map.95 = (bf16[32,4096]{1,0:T(8,128)(2,1)}, bf16[32,4096]{1,0:T(8,128)(2,1)}, bf16[32,4096]{1,0:T(8,128)(2,1)}, bf16[32,4096]{1,0:T(8,128)(2,1)}) custom-call(bf16[32,4,32,128]{3,2,1,0:T(8,128)(2,1)S(1)} %all_to_all.11.packed), custom_call_target="tpu_custom_call" | custom-call | tf_op jit(solution)/shard_map/pallas_call | solution.py:91

commit v6 on v4

--- a/solution.py
+++ b/solution.py
@@ -174,9 +174,6 @@
     turns = queries // QUERY_TILE
     factor = SCALE * math.log2(math.e)
     list_bias(random_ref, global_ref, bias_ref)
-    flip(v_at, vt_ref, keys)
-    vt_ref[HEAD_DIM:, :] = jnp.ones_like(vt_ref[HEAD_DIM:, :])
-
     def through(left_ref, right_ref, here):
         def add(c, total):
             at = span(c, KEY_TILE)
@@ -216,41 +213,57 @@
 
         each(steps, one, 0)
 
-    def mix(t):
-        here = span(t, QUERY_TILE)
-        mixed = through(vt_ref, w_ref, here)
-        inverse = 1.0 / mixed[HEAD_DIM : HEAD_DIM + 1]
-        out = (mixed[:HEAD_DIM] * inverse).astype(jnp.bfloat16).astype(jnp.float32)
-        put(out_at, t * QUERY_TILE, out.T)
-        g = tile_of(g_at, t * QUERY_TILE, QUERY_TILE).astype(jnp.float32).T
-        delta_ref[:, here] = jnp.sum(g * out, axis=0, keepdims=True) * inverse
-        g = g * inverse
-        gt_ref[:, here] = g.astype(gt_ref.dtype)
-        gs_ref[here, :] = g.T.astype(gs_ref.dtype)
-
+    every = range(turns)
+    places = [span(t, QUERY_TILE) for t in every]
     tops = [score(0)]
-    for t in range(turns):
+    flip(v_at, vt_ref, keys)
+    vt_ref[HEAD_DIM:, :] = jnp.ones_like(vt_ref[HEAD_DIM:, :])
+    for t in every:
         if t + 1 < turns:
             tops.append(score(t + 1))
         weigh(t, tops[t])
-        mix(t)
-
-    def backward(c, _):
+
+    grads = [tile_of(g_at, t * QUERY_TILE, QUERY_TILE).astype(jnp.float32).T for t in every]
+    mixed = [through(vt_ref, w_ref, here) for here in places]
+    inverse = [1.0 / x[HEAD_DIM : HEAD_DIM + 1] for x in mixed]
+    outs = [(x[:HEAD_DIM] * i).astype(jnp.bfloat16) for x, i in zip(mixed, inverse)]
+    scaled = [g * i for g, i in zip(grads, inverse)]
+    for here, g in zip(places, scaled):
+        gt_ref[:, here] = g.astype(gt_ref.dtype)
+    for here, g, out in zip(places, scaled, outs):
+        delta_ref[:, here] = jnp.sum(g * out.astype(jnp.float32), axis=0, keepdims=True)
+    for here, g in zip(places, scaled):
+        gs_ref[here, :] = g.T.astype(gs_ref.dtype)
+
+    def values_step(c, _):
+        put(dv_at, c * KEY_TILE, dot(w_ref[span(c, KEY_TILE), :], gs_ref[...]))
+        return 0
+
+    def score_grad_step(c, _):
         at = span(c, KEY_TILE)
-        put(dv_at, c * KEY_TILE, dot(w_ref[at, :], gs_ref[...]))
         v = tile_of(v_at, c * KEY_TILE, KEY_TILE)
-        for t in range(turns):
-            here = span(t, QUERY_TILE)
+        for here in places:
             gap = dot(v, gt_ref[:, here]) - delta_ref[:, here]
             ds_ref[at, here] = (w_ref[at, here].astype(jnp.float32) * gap).astype(ds_ref.dtype)
+        return 0
+
+    def keys_step(c, _):
         q = tile_of(q_at, 0, queries)
-        put(dk_at, c * KEY_TILE, dot(ds_ref[at, :], q) * SCALE)
+        put(dk_at, c * KEY_TILE, dot(ds_ref[span(c, KEY_TILE), :], q) * SCALE)
         return 0
 
-    each(steps, backward, 0)
+    if ds_ref is w_ref:
+        each(steps, values_step, 0)
+    each(steps, score_grad_step, 0)
     flip(k_at, kt_ref, keys)
-    for t in range(turns):
-        put(dq_at, t * QUERY_TILE, (through(kt_ref, ds_ref, span(t, QUERY_TILE)) * SCALE).T)
+    for t, out in zip(every, outs):
+        put(out_at, t * QUERY_TILE, out.astype(jnp.float32).T)
+    if ds_ref is not w_ref:
+        each(steps, values_step, 0)
+    sums = [through(kt_ref, ds_ref, here) * SCALE for here in places]
+    each(steps, keys_step, 0)
+    for t, dq in zip(every, sums):
+        put(dq_at, t * QUERY_TILE, dq.T)
 
 
 def attend(rows, wide, random_blocks, global_blocks, order):

time: 69.6 us -> 69.7 us (level)
  no operation moved by 1% of the time
where the time goes in v6:
time: 69.7 us; the launch traced here: 69.5 us
  blocking collectives  62.6 us (90%)
  Pallas kernels  6.24 us (9%)
    all_to_all x1, blocking collectives, body(): got = trade(sent)  33.3 us
    all_to_all x1, blocking collectives, body(): return tuple(unpack(trade(back)))  29.3 us
    pallas_call x1, Pallas kernels, attend(): pl.pallas_call(kernel, out_shape=outs, in_specs=[WHOLE] * len(ins), out_s...  3.92 us

profile of v6, /device:TPU:1, one launch (start us, length us, event | category | flops | bytes accessed | tf_op | source)
XLA Modules:
  0.0 69.5 jit_solution(11979911022180745950)
XLA Ops:
  0.6 1.3 %shard_map.93 = (bf16[32,4,32,128]{3,2,1,0:T(8,128)(2,1)S(1)}, s32[3,16,32]{2,1,0:T(8,128)S(1)}, s32[1,2]{1,0:T(1,128)S(1)}) custom-call(s32[3,16,32]{2,1,0:T(8,128)} %bitcast.2, s32[1,2]{1,0:T(1,128)} %bitcast.3, bf16[32,4096]{1,0:T(8,128)(2,1)} %refs_0_.1, bf16[32,4096]{1,0:T(8,128)(2,1)} %refs_1_.1, bf16[32,4096]{1,0:T(8,128)(2,1)} %refs_2_.1, ...), custom_call_target="tpu_custom_call" | custom-call | tf_op jit(solution)/shard_map/pallas_call | solution.py:65
  1.9 33.3 %all_to_all.10.refs_0_ = bf16[32,4,32,128]{3,2,1,0:T(8,128)(2,1)S(1)} all-to-all(bf16[32,4,32,128]{3,2,1,0:T(8,128)(2,1)S(1)} %get-tuple-element.7), channel_id=1, replica_groups=mesh['seq'=8,'head'=4] {'seq':(4)2,'head','seq':(1)4}, dimensions={0} | all-to-all | bytes 2097152 | tf_op jit(solution)/shard_map/all_to_all | solution.py:321
  35.2 3.9 %shard_map.94 = bf16[32,4,32,128]{3,2,1,0:T(8,128)(2,1)S(1)} custom-call(bf16[32,4,32,128]{3,2,1,0:T(8,128)(2,1)S(1)} %all_to_all.10.refs_0_, s32[3,16,32]{2,1,0:T(8,128)S(1)} %get-tuple-element.8.refs_1_, s32[1,2]{1,0:T(1,128)S(1)} %get-tuple-element.9.refs_2_), custom_call_target="tpu_custom_call" | custom-call | tf_op jit(solution)/shard_map/pallas_call | solution.py:296
  39.1 29.3 %all_to_all.11.packed = bf16[32,4,32,128]{3,2,1,0:T(8,128)(2,1)S(1)} all-to-all(bf16[32,4,32,128]{3,2,1,0:T(8,128)(2,1)S(1)} %shard_map.94), channel_id=1, replica_groups=mesh['seq'=8,'head'=4] {'seq':(4)2,'head','seq':(1)4}, dimensions={0} | all-to-all | bytes 2097152 | tf_op jit(solution)/shard_map/all_to_all | solution.py:329
  68.4 1.0 %shard_map.95 = (bf16[32,4096]{1,0:T(8,128)(2,1)}, bf16[32,4096]{1,0:T(8,128)(2,1)}, bf16[32,4096]{1,0:T(8,128)(2,1)}, bf16[32,4096]{1,0:T(8,128)(2,1)}) custom-call(bf16[32,4,32,128]{3,2,1,0:T(8,128)(2,1)S(1)} %all_to_all.11.packed), custom_call_target="tpu_custom_call" | custom-call | tf_op jit(solution)/shard_map/pallas_call | solution.py:91

commit v7 on v5

--- a/solution.py
+++ b/solution.py
@@ -13,7 +13,7 @@
 BLOCK = 64
 SCALE = HEAD_DIM**-0.5
 QUERY_TILE = 256
-KEY_TILE = 1024
+KEY_TILE = 256
 FAR_LANES = 4
 
 WHOLE = pl.BlockSpec(memory_space=pltpu.VMEM)

time: 69.6 us -> 69.8 us (level)
  no operation moved by 1% of the time
where the time goes in v7:
time: 69.8 us; the launch traced here: 69.6 us
  blocking collectives  62.6 us (90%)
  Pallas kernels  6.38 us (9%)
    all_to_all x1, blocking collectives, body(): got = trade(sent)  33.3 us
    all_to_all x1, blocking collectives, body(): return tuple(unpack(trade(back)))  29.3 us
    pallas_call x1, Pallas kernels, attend(): pl.pallas_call(kernel, out_shape=outs, in_specs=[WHOLE] * len(ins), out_s...  4.05 us

profile of v7, /device:TPU:1, one launch (start us, length us, event | category | flops | bytes accessed | tf_op | source)
XLA Modules:
  0.0 69.6 jit_solution(6346621507825571665)
XLA Ops:
  0.6 1.3 %shard_map.93 = (bf16[32,4,32,128]{3,2,1,0:T(8,128)(2,1)S(1)}, s32[3,16,32]{2,1,0:T(8,128)S(1)}, s32[1,2]{1,0:T(1,128)S(1)}) custom-call(s32[3,16,32]{2,1,0:T(8,128)} %bitcast.2, s32[1,2]{1,0:T(1,128)} %bitcast.3, bf16[32,4096]{1,0:T(8,128)(2,1)} %refs_0_.1, bf16[32,4096]{1,0:T(8,128)(2,1)} %refs_1_.1, bf16[32,4096]{1,0:T(8,128)(2,1)} %refs_2_.1, ...), custom_call_target="tpu_custom_call" | custom-call | tf_op jit(solution)/shard_map/pallas_call | solution.py:65
  1.9 33.3 %all_to_all.10.refs_0_ = bf16[32,4,32,128]{3,2,1,0:T(8,128)(2,1)S(1)} all-to-all(bf16[32,4,32,128]{3,2,1,0:T(8,128)(2,1)S(1)} %get-tuple-element.7), channel_id=1, replica_groups=mesh['seq'=8,'head'=4] {'seq':(4)2,'head','seq':(1)4}, dimensions={0} | all-to-all | bytes 2097152 | tf_op jit(solution)/shard_map/all_to_all | solution.py:308
  35.2 4.1 %shard_map.94 = bf16[32,4,32,128]{3,2,1,0:T(8,128)(2,1)S(1)} custom-call(bf16[32,4,32,128]{3,2,1,0:T(8,128)(2,1)S(1)} %all_to_all.10.refs_0_, s32[3,16,32]{2,1,0:T(8,128)S(1)} %get-tuple-element.8.refs_1_, s32[1,2]{1,0:T(1,128)S(1)} %get-tuple-element.9.refs_2_), custom_call_target="tpu_custom_call" | custom-call | tf_op jit(solution)/shard_map/pallas_call | solution.py:283
  39.3 29.3 %all_to_all.11.packed = bf16[32,4,32,128]{3,2,1,0:T(8,128)(2,1)S(1)} all-to-all(bf16[32,4,32,128]{3,2,1,0:T(8,128)(2,1)S(1)} %shard_map.94), channel_id=1, replica_groups=mesh['seq'=8,'head'=4] {'seq':(4)2,'head','seq':(1)4}, dimensions={0} | all-to-all | bytes 2097152 | tf_op jit(solution)/shard_map/all_to_all | solution.py:316
  68.6 1.0 %shard_map.95 = (bf16[32,4096]{1,0:T(8,128)(2,1)}, bf16[32,4096]{1,0:T(8,128)(2,1)}, bf16[32,4096]{1,0:T(8,128)(2,1)}, bf16[32,4096]{1,0:T(8,128)(2,1)}) custom-call(bf16[32,4,32,128]{3,2,1,0:T(8,128)(2,1)S(1)} %all_to_all.11.packed), custom_call_target="tpu_custom_call" | custom-call | tf_op jit(solution)/shard_map/pallas_call | solution.py:91
